TPU v7x, 32 devices: a whole 2x2x4 slice. The times are simulated.
32 devices in a mesh: row: 16 (over z, y, x), col: 2 (over core).
Axes of the slice: x: 2, y: 2, z: 4, core: 2. Of those that a mesh axis runs over, the one named last changes fastest.
Arguments:
- density: bfloat16 [256, 64, 1024], P('row', None, 'col'), may hold values from -0.9 to 1.9
- columns: int32 [256, 16], replicated, may hold values from 0 to 255, as said below
Outputs:
- purified: float32 [256, 64, 1024], P('row', None, 'col')
Inputs may be any that keep to these rules, and one draw needn't show every extreme that they name: Stored block a of row i lies in group a // 8: columns[i, a] is congruent to a // 8 modulo 2. The columns of a row are distinct and lie within cyclic distance 48 of i; row 0 always stores a block at distance exactly 48, and other rows may as well. The diagonal column i stands in slot (i mod 2) * 8.
All inputs are finite; a program needn't handle non-finite values.
Results may differ from a plain program's by a relative error of at most 0.0034.
Values may be sent and summed in bfloat16 or wider, within the bound.
A program may use at most 128 MiB of HBM per device.

v0:
```python
import jax
import jax.numpy as jnp
from jax import lax
from jax.sharding import PartitionSpec as P

SPAN = 3


def passed_along(block, axis, distance):
    devices = range(lax.axis_size(axis))
    route = [((i - distance) % len(devices), i) for i in devices]
    return lax.ppermute(block, axis, route)


def fetch_panels(density):
    panels = []
    for offset in range(-SPAN, SPAN + 1):
        if offset == 0:
            panels.append(density)
        else:
            panels.append(passed_along(density, "row", -offset))
    return panels


def make_accumulate(table, flat_index, live):

    def accumulate(total, piece, start):
        width = table.shape[1]
        count = piece.shape[2] // width
        chosen = jnp.take(table, flat_index, axis=0)
        chosen = jnp.where(live[..., None, None], chosen, jnp.zeros((), table.dtype))
        left = piece.reshape(piece.shape[0], width, count, width)
        part = jnp.einsum("ixby,iabyz->ixaz", left, chosen, preferred_element_type=jnp.float32)
        return part.reshape(total.shape)

    return accumulate


def shards(density, columns):
    row_index = lax.axis_index("row")
    col_index = lax.axis_index("col")
    local_rows = density.shape[0]
    width = density.shape[1]
    group_size = density.shape[2] // width
    total = columns.shape[0]
    panel_count = 2 * SPAN + 1
    base = row_index * local_rows
    own_columns = lax.dynamic_slice_in_dim(columns, base, local_rows, 0)
    group_columns = lax.dynamic_slice_in_dim(own_columns, col_index * group_size, group_size, 1)
    distance = jnp.mod(own_columns - base + total // 2, total) - total // 2
    owner = jnp.floor_divide(distance, local_rows)
    inner = distance - owner * local_rows
    panel_row = (owner + SPAN) * local_rows + inner
    shifts = jnp.arange(panel_count, dtype=jnp.int32)[:, None] - SPAN
    within = jnp.arange(local_rows, dtype=jnp.int32)[None, :]
    global_rows = jnp.mod(base + shifts * local_rows + within, total).reshape(-1)
    panel_columns = jnp.take(columns, global_rows, axis=0)
    panel_columns = lax.dynamic_slice_in_dim(panel_columns, col_index * group_size, group_size, 1)
    candidates = jnp.take(panel_columns, panel_row, axis=0)
    equal = candidates[:, None, :, :] == group_columns[:, :, None, None]
    live = jnp.any(equal, axis=-1)
    slots = jnp.arange(group_size, dtype=jnp.int32)
    chosen_slot = jnp.sum(jnp.where(equal, slots, 0), axis=-1)
    flat_index = panel_row[:, None, :] * group_size + chosen_slot
    panels = fetch_panels(density)
    stacked = jnp.stack(panels)
    table = stacked.reshape(panel_count, local_rows, width, group_size, width)
    table = table.transpose(0, 1, 3, 2, 4).reshape(
        panel_count * local_rows * group_size, width, width
    )
    accumulate = make_accumulate(table, flat_index, live)
    empty = jnp.zeros(density.shape, jnp.float32)
    square = accumulate(
        empty, lax.all_gather(density, "col", axis=2, tiled=True), jnp.int32(0)
    ).astype(jnp.bfloat16)
    cube = accumulate(empty, lax.all_gather(square, "col", axis=2, tiled=True), jnp.int32(0))
    return 3.0 * square.astype(jnp.float32) - 2.0 * cube


def solution(mesh):
    placed = (P("row", None, "col"), P())
    return jax.shard_map(
        shards, mesh=mesh, in_specs=placed, out_specs=P("row", None, "col"), check_vma=False
    )
```

profile of v0, /device:TPU:0, one launch (start us, length us, event | category | flops | bytes accessed | tf_op | source)
XLA Modules:
  0.0 263.6 jit_solution(6076021142942341352)
XLA Ops:
  6.5 0.0 all-gather.3.cloned.1.call-start
  6.5 3.9 %collective-permute-start = (bf16[16,64,512]{2,1,0:T(8,128)(2,1)}, bf16[16,64,512]{2,1,0:T(8,128)(2,1)S(1)}, u32[]{:S(2)}, u32[]{:S(2)}) collective-permute-start(bf16[16,64,512]{2,1,0:T(8,128)(2,1)} %param.4), channel_id=1, source_target_pairs={{26,0},{28,2},{30,4},{0,6},{2,8},{4,10},{6,12},{8,14},{10,16},{12,... | collective-permute-start | bytes 3145736 | tf_op jit(solution)/shard_map/ppermute | solution.py:12
  10.4 1.5 collective-permute-start.1
  12.0 0.6 collective-permute-start.2
  12.5 5.0 %collective-permute-start.3 = (bf16[16,64,512]{2,1,0:T(8,128)(2,1)}, bf16[16,64,512]{2,1,0:T(8,128)(2,1)}, u32[]{:S(2)}, u32[]{:S(2)}) collective-permute-start(bf16[16,64,512]{2,1,0:T(8,128)(2,1)} %param.4), channel_id=1, source_target_pairs={{2,0},{4,2},{6,4},{8,6},{10,8},{12,10},{14,12},{16,14},{18,16},{20... | collective-permute-start | bytes 3145736 | tf_op jit(solution)/shard_map/ppermute | solution.py:12
  17.6 0.5 collective-permute-start.4
  18.1 0.0 all-gather.3.cloned.1.call-update
  18.1 0.0 all-gather.5.cloned.1.call-start
  18.2 0.8 broadcast_multiply_fusion
  19.0 0.1 iota_add_fusion
  19.1 0.8 copy.28
  19.9 0.1 add.148
  20.0 0.1 add.145
  20.0 0.1 copy.29
  20.1 0.1 reshape.148
  20.2 0.1 copy.27
  20.3 0.6 gather_fusion
  21.0 0.1 dynamic-slice_select_fusion
  21.1 0.7 gather_fusion.1
  21.8 54.2 %collective-permute-done = bf16[16,64,512]{2,1,0:T(8,128)(2,1)S(1)} collective-permute-done((bf16[16,64,512]{2,1,0:T(8,128)(2,1)}, bf16[16,64,512]{2,1,0:T(8,128)(2,1)S(1)}, u32[]{:S(2)}, u32[]{:S(2)}) %collective-permute-start) | collective-permute-done | bytes 1048608 | tf_op jit(solution)/shard_map/ppermute | solution.py:12
  76.0 0.0 collective-permute-start.5
  76.0 0.1 broadcast_select_fusion
  76.1 0.9 copy-done.5
  77.0 2.8 %stack.27 = bf16[1,16,64,8,64]{4,3,2,1,0:T(8,128)(2,1)S(1)} reshape(bf16[16,64,512]{2,1,0:T(8,128)(2,1)} %param.4) | data formatting | bytes 2097152 | tf_op jit(solution)/shard_map/stack | solution.py:66
  79.8 0.1 copy.30
  79.9 0.8 dynamic_slice.11
  80.7 0.1 copy.31
  80.8 0.1 copy.32
  80.8 0.2 fusion.12
  81.1 0.1 reshape.158
  81.2 0.3 compare_reduce_fusion
  81.5 3.9 %stack.24 = bf16[1,16,64,8,64]{4,3,2,1,0:T(8,128)(2,1)} reshape(bf16[16,64,512]{2,1,0:T(8,128)(2,1)} %copy-done.5) | data formatting | bytes 2097152 | tf_op jit(solution)/shard_map/stack | solution.py:66
  85.4 3.5 %copy_dynamic-update-slice_fusion.6 = bf16[7,16,64,8,64]{4,2,3,1,0:T(8,128)(2,1)} fusion(bf16[1,16,64,8,64]{4,3,2,1,0:T(8,128)(2,1)} %stack.24), kind=kLoop, calls=%fused_computation.20 | loop fusion | bytes 3145728
  88.9 0.0 collective-permute-done.1
  88.9 3.9 %stack.25 = bf16[1,16,64,8,64]{4,3,2,1,0:T(8,128)(2,1)} reshape(bf16[16,64,512]{2,1,0:T(8,128)(2,1)} %collective-permute-done.1) | data formatting | bytes 2097152 | tf_op jit(solution)/shard_map/stack | solution.py:66
  92.8 27.0 %collective-permute-done.2 = bf16[16,64,512]{2,1,0:T(8,128)(2,1)} collective-permute-done((bf16[16,64,512]{2,1,0:T(8,128)(2,1)}, bf16[16,64,512]{2,1,0:T(8,128)(2,1)}, u32[]{:S(2)}, u32[]{:S(2)}) %collective-permute-start.2) | collective-permute-done | bytes 1048608 | tf_op jit(solution)/shard_map/ppermute | solution.py:12
  119.8 3.9 %stack.26 = bf16[1,16,64,8,64]{4,3,2,1,0:T(8,128)(2,1)} reshape(bf16[16,64,512]{2,1,0:T(8,128)(2,1)} %collective-permute-done.2) | data formatting | bytes 2097152 | tf_op jit(solution)/shard_map/stack | solution.py:66
  123.8 0.0 collective-permute-done.3
  123.8 3.9 %stack.28 = bf16[1,16,64,8,64]{4,3,2,1,0:T(8,128)(2,1)} reshape(bf16[16,64,512]{2,1,0:T(8,128)(2,1)} %collective-permute-done.3) | data formatting | bytes 2097152 | tf_op jit(solution)/shard_map/stack | solution.py:66
  127.6 0.0 collective-permute-done.4
  127.6 2.1 stack.29
  129.7 0.0 collective-permute-done.5
  129.7 3.9 %stack.30 = bf16[1,16,64,8,64]{4,3,2,1,0:T(8,128)(2,1)} reshape(bf16[16,64,512]{2,1,0:T(8,128)(2,1)} %collective-permute-done.5) | data formatting | bytes 2097152 | tf_op jit(solution)/shard_map/stack | solution.py:66
  133.6 3.7 %copy_dynamic-update-slice_fusion.5 = bf16[7,16,64,8,64]{4,2,3,1,0:T(8,128)(2,1)} fusion(bf16[7,16,64,8,64]{4,2,3,1,0:T(8,128)(2,1)} %copy_dynamic-update-slice_fusion.6, bf16[1,16,64,8,64]{4,3,2,1,0:T(8,128)(2,1)} %stack.25), kind=kLoop, calls=%fused_computation.19 | loop fusion | bytes 4194304
  137.4 0.0 copy-done.2
  137.4 1.9 copy_dynamic-update-slice_fusion.4
  139.3 1.9 copy_dynamic-update-slice_fusion.3
  141.2 0.0 copy-done.1
  141.2 2.0 copy_dynamic-update-slice_fusion.2
  143.2 0.0 copy-done.3
  143.2 1.9 copy_dynamic-update-slice_fusion.1
  145.1 0.0 copy-done.4
  145.1 2.0 copy_dynamic-update-slice_fusion
  147.1 31.6 %gather_fusion.2 = bf16[2048,64,64]{2,1,0:T(8,128)(2,1)} fusion(bf16[896,64,64]{2,1,0:T(8,128)(2,1)} %bitcast.20, s32[2048]{0:T(1024)S(1)} %broadcast_clamp_fusion), kind=kCustom, calls=%fused_computation.clone | custom fusion | bytes 33562624 | tf_op jit(solution)/shard_map/jit(_take)/gather | solution.py:30
  178.6 6.3 %reshape.128 = bf16[16,64,16,64]{3,2,1,0:T(8,128)(2,1)} reshape(bf16[16,64,1024]{2,1,0:T(8,128)(2,1)} %all-gather.3.cloned.1.call-done) | data formatting | bytes 4194304 | tf_op jit(solution)/shard_map/reshape | solution.py:32
  185.0 21.4 %bitcast_convert_fusion = bf16[16,8,64,64]{3,2,1,0:T(8,128)(2,1)S(1)} fusion(bf16[16,64,16,64,1]{3,2,1,0,4:T(8,128)(2,1)} %bitcast.24, bf16[16,8,16,64,64]{4,3,2,1,0:T(8,128)(2,1)} %bitcast.21, pred[16,8,16]{2,1,0:T(8,128)(4,1)S(1)} %get-tuple-element.6, pred[16,8,16]{2,1,0:T(8,128)(4,1)S(1)} %compare_reduce_fusion), kind=kOutput, calls=%fused_computation.12 | convolution fusion | flops 1091043328 | bytes 19927040 | tf_op jit(solution)/shard_map/ixby,iabyz->ixaz/dot_general | solution.py:33
  206.4 1.8 copy.42
  208.2 0.0 all-gather.5.cloned.1.call-update
  208.2 15.3 %all-gather.5.cloned.1.call-done = bf16[16,64,1024]{2,1,0:T(8,128)(2,1)} async-done(((bf16[16,64,512]{2,1,0:T(8,128)(2,1)}), bf16[16,64,1024]{2,1,0:T(8,128)(2,1)}) %all-gather.5.cloned.1.call-update) | async-done | bytes 2097168 | tf_op jit(solution)/shard_map/all_gather | solution.py:76
  223.5 6.3 %reshape.129 = bf16[16,64,16,64]{3,2,1,0:T(8,128)(2,1)} reshape(bf16[16,64,1024]{2,1,0:T(8,128)(2,1)} %all-gather.5.cloned.1.call-done) | data formatting | bytes 4194304 | tf_op jit(solution)/shard_map/reshape | solution.py:32
  229.8 16.3 %bitcast_multiply_fusion = f32[16,64,8,64]{3,1,2,0:T(8,128)S(1)} fusion(bf16[16,8,16,64,64]{4,3,2,1,0:T(8,128)(2,1)} %bitcast.22, pred[16,8,16]{2,1,0:T(8,128)(4,1)S(1)} %get-tuple-element.6, pred[16,8,16]{2,1,0:T(8,128)(4,1)S(1)} %compare_reduce_fusion, bf16[16,64,16,64,1]{3,2,1,0,4:T(8,128)(2,1)} %bitcast.23), kind=kOutput, calls=%fused_computation.10 | convolution fusion | flops 1091043328 | bytes 20975616 | tf_op jit(solution)/shard_map/ixby,iabyz->ixaz/dot_general | solution.py:33
  246.2 5.2 %copy.45 = f32[16,64,8,64]{3,2,1,0:T(8,128)} copy(f32[16,64,8,64]{3,1,2,0:T(8,128)S(1)} %bitcast_multiply_fusion) | data formatting | bytes 4194304 | tf_op jit(solution)/shard_map/mul | solution.py:77
  251.4 3.5 %mul.54 = f32[16,64,512]{2,1,0:T(8,128)S(1)} reshape(f32[16,64,8,64]{3,2,1,0:T(8,128)} %copy.45) | data formatting | bytes 4194304 | tf_op jit(solution)/shard_map/mul | solution.py:77
  255.0 1.8 multiply_subtract_fusion
  (16 shorter events, 0.1 us)
Async XLA Ops:
  6.5 172.1 %all-gather.3.cloned.1.call-start = ((), (), s32[]{:S(2)}) async-start(), calls=%async_computation | async-start | bytes 3145728 | tf_op jit(solution)/shard_map/all_gather | solution.py:74
  6.5 69.5 %collective-permute-start = (bf16[16,64,512]{2,1,0:T(8,128)(2,1)}, bf16[16,64,512]{2,1,0:T(8,128)(2,1)S(1)}, u32[]{:S(2)}, u32[]{:S(2)}) collective-permute-start(bf16[16,64,512]{2,1,0:T(8,128)(2,1)} %param.4), channel_id=1, source_target_pairs={{26,0},{28,2},{30,4},{0,6},{2,8},{4,10},{6,12},{8,14},{10,16},{12,... | collective-permute-start | bytes 3145736 | tf_op jit(solution)/shard_map/ppermute | solution.py:12
  10.4 78.5 %collective-permute-start.1 = (bf16[16,64,512]{2,1,0:T(8,128)(2,1)}, bf16[16,64,512]{2,1,0:T(8,128)(2,1)}, u32[]{:S(2)}, u32[]{:S(2)}) collective-permute-start(bf16[16,64,512]{2,1,0:T(8,128)(2,1)} %param.4), channel_id=1, source_target_pairs={{28,0},{30,2},{0,4},{2,6},{4,8},{6,10},{8,12},{10,14},{12,16},{14,... | collective-permute-start | bytes 3145736 | tf_op jit(solution)/shard_map/ppermute | solution.py:12
  12.0 107.9 %collective-permute-start.2 = (bf16[16,64,512]{2,1,0:T(8,128)(2,1)}, bf16[16,64,512]{2,1,0:T(8,128)(2,1)}, u32[]{:S(2)}, u32[]{:S(2)}) collective-permute-start(bf16[16,64,512]{2,1,0:T(8,128)(2,1)} %param.4), channel_id=1, source_target_pairs={{30,0},{0,2},{2,4},{4,6},{6,8},{8,10},{10,12},{12,14},{14,16},{16,... | collective-permute-start | bytes 3145736 | tf_op jit(solution)/shard_map/ppermute | solution.py:12
  12.5 111.2 %collective-permute-start.3 = (bf16[16,64,512]{2,1,0:T(8,128)(2,1)}, bf16[16,64,512]{2,1,0:T(8,128)(2,1)}, u32[]{:S(2)}, u32[]{:S(2)}) collective-permute-start(bf16[16,64,512]{2,1,0:T(8,128)(2,1)} %param.4), channel_id=1, source_target_pairs={{2,0},{4,2},{6,4},{8,6},{10,8},{12,10},{14,12},{16,14},{18,16},{20... | collective-permute-start | bytes 3145736 | tf_op jit(solution)/shard_map/ppermute | solution.py:12
  17.6 110.1 %collective-permute-start.4 = (bf16[16,64,512]{2,1,0:T(8,128)(2,1)}, bf16[16,64,512]{2,1,0:T(8,128)(2,1)S(1)}, u32[]{:S(2)}, u32[]{:S(2)}) collective-permute-start(bf16[16,64,512]{2,1,0:T(8,128)(2,1)} %param.4), channel_id=1, source_target_pairs={{4,0},{6,2},{8,4},{10,6},{12,8},{14,10},{16,12},{18,14},{20,16},{2... | collective-permute-start | bytes 3145736 | tf_op jit(solution)/shard_map/ppermute | solution.py:12
  18.1 205.4 %all-gather.5.cloned.1.call-start = ((), (), s32[]{:S(2)}) async-start(), calls=%async_computation.1 | async-start | bytes 3145728 | tf_op jit(solution)/shard_map/all_gather | solution.py:76
  76.0 1.0 copy-start.5
  76.0 53.7 %collective-permute-start.5 = (bf16[16,64,512]{2,1,0:T(8,128)(2,1)}, bf16[16,64,512]{2,1,0:T(8,128)(2,1)}, u32[]{:S(2)}, u32[]{:S(2)}) collective-permute-start(bf16[16,64,512]{2,1,0:T(8,128)(2,1)} %param.4), channel_id=1, source_target_pairs={{6,0},{8,2},{10,4},{12,6},{14,8},{16,10},{18,12},{20,14},{22,16},{... | collective-permute-start | bytes 3145736 | tf_op jit(solution)/shard_map/ppermute | solution.py:12
  133.6 3.7 %copy-start.2 = (bf16[1,16,64,8,64]{4,3,2,1,0:T(8,128)(2,1)S(1)}, bf16[1,16,64,8,64]{4,3,2,1,0:T(8,128)(2,1)}, u32[]{:S(2)}) copy-start(bf16[1,16,64,8,64]{4,3,2,1,0:T(8,128)(2,1)} %stack.26) | copy-start | bytes 3145732
  137.4 3.9 %copy-start.1 = (bf16[1,16,64,8,64]{4,3,2,1,0:T(8,128)(2,1)S(1)}, bf16[1,16,64,8,64]{4,3,2,1,0:T(8,128)(2,1)}, u32[]{:S(2)}) copy-start(bf16[1,16,64,8,64]{4,3,2,1,0:T(8,128)(2,1)} %stack.28) | copy-start | bytes 3145732
  139.3 3.9 %copy-start.3 = (bf16[1,16,64,8,64]{4,3,2,1,0:T(8,128)(2,1)S(1)}, bf16[1,16,64,8,64]{4,3,2,1,0:T(8,128)(2,1)}, u32[]{:S(2)}) copy-start(bf16[1,16,64,8,64]{4,3,2,1,0:T(8,128)(2,1)} %stack.29) | copy-start | bytes 3145732
  141.2 3.9 %copy-start.4 = (bf16[1,16,64,8,64]{4,3,2,1,0:T(8,128)(2,1)S(1)}, bf16[1,16,64,8,64]{4,3,2,1,0:T(8,128)(2,1)}, u32[]{:S(2)}) copy-start(bf16[1,16,64,8,64]{4,3,2,1,0:T(8,128)(2,1)} %stack.30) | copy-start | bytes 3145732
  251.4 3.5 %copy-start = (bf16[16,64,512]{2,1,0:T(8,128)(2,1)S(1)}, bf16[16,64,512]{2,1,0:T(8,128)(2,1)}, u32[]{:S(2)}) copy-start(bf16[16,64,512]{2,1,0:T(8,128)(2,1)} %copy.42) | copy-start | bytes 3145732
Sparse Core Ops, SparseCore 0:
  18.2 8.1 all-gather.2
  208.3 15.1 all-gather.4
where the time goes:
time: 265 us; the launch traced here: 264 us
  local copies, waits for them, and re-layouts  101 us (38%)
  waiting for transfers between devices  96.6 us (36%)
  matrix products  37.7 us (14%)
  between operations  13.5 us (5%)
  starting transfers between devices  11.6 us (4%)
  other arithmetic  3.43 us (1%)
    ppermute x6, waiting for transfers between devices, passed_along(): return lax.ppermute(block, axis, route)  81.3 us
    dot_general x2, matrix products, accumulate(): jnp.einsum('ixby,iabyz->ixaz', left, chosen, preferred_element_type=jnp.f...  37.7 us
    gather x1, local copies, waits for them, and re-layouts, accumulate(): chosen = jnp.take(table, flat_index, axis=0)  31.6 us
    another operation x8, local copies, waits for them, and re-layouts, shards(): stacked = jnp.stack(panels)  26.3 us
    unnamed x19, local copies, waits for them, and re-layouts  16.7 us
    all_gather x1, waiting for transfers between devices, shards(): lax.all_gather(square, 'col', axis=2, tiled=True)  15.3 us
    reshape x2, local copies, waits for them, and re-layouts, accumulate(): left = piece.reshape(piece.shape[0], width, count, width)  12.7 us
    ppermute x6, starting transfers between devices, passed_along(): return lax.ppermute(block, axis, route)  11.5 us
  transfers between devices with their start and end apart: 8, of which 3 were waited for; matrix products, arithmetic and copies ran while one was open for 30% of the time, Pallas kernels for 0%

commit v1 on v0

v1 whole, which is shorter than its diff:
```python
import functools

import jax
import jax.numpy as jnp
from jax import lax
from jax.experimental import pallas as pl
from jax.experimental.pallas import tpu as pltpu
from jax.sharding import PartitionSpec as P

REACH = 48
UNROLL = 4


def passed_along(block, axis, distance):
    size = lax.axis_size(axis)
    route = [((i - distance) % size, i) for i in range(size)]
    return lax.ppermute(block, axis, route)


def live_list(columns, rows, width, group_size, span):
    total, stored = columns.shape
    base = lax.axis_index("row") * rows
    first = lax.axis_index("col") * group_size
    own = lax.dynamic_slice_in_dim(columns, base, rows, 0)
    wanted = lax.dynamic_slice_in_dim(own, first, group_size, 1)
    group = lax.dynamic_slice_in_dim(columns, first, group_size, 1)
    candidates = jnp.take(group, own, axis=0)
    distance = jnp.mod(own - base + span * rows, total)
    equal = candidates[:, :, :, None] == wanted[:, None, None, :]
    slots = jnp.arange(group_size, dtype=jnp.int32)
    live = jnp.any(equal, axis=-1)
    place = jnp.sum(jnp.where(equal, slots, 0), axis=-1)
    inner = jnp.arange(stored, dtype=jnp.int32)[None, :, None]
    code = ((distance[:, :, None] * group_size + slots) * stored + inner) * group_size + place
    flat = live.reshape(rows, stored * group_size)
    code = code.reshape(rows, stored * group_size)
    order = jnp.cumsum(flat.astype(jnp.int32), axis=1)
    ranks = jnp.arange(1, stored * group_size + 1, dtype=jnp.int32)
    chosen = flat[:, None, :] & (order[:, None, :] == ranks[None, :, None])
    packed = jnp.sum(jnp.where(chosen, code[:, None, :] + 1, 0), axis=-1)
    return order[:, -1], packed - 1


def first_kernel(stored, group_size, width, count_ref, code_ref, panels_ref, left_ref, right_ref, square_ref):
    row = pl.program_id(0)
    right_ref[...] = jnp.zeros_like(right_ref)
    half = lax.broadcasted_iota(jnp.int32, (width, 2 * width), 1) >= width

    def one(entry, carry):
        pieces = []
        for part in range(UNROLL):
            raw = code_ref[row, entry * UNROLL + part]
            real = raw >= 0
            code = jnp.maximum(raw, 0)
            place = lax.rem(code, group_size)
            code = lax.div(code, group_size)
            inner = lax.rem(code, stored)
            code = lax.div(code, stored)
            slot = lax.rem(code, group_size)
            source = lax.div(code, group_size)
            lanes = pl.ds(pl.multiple_of(lax.div(slot, 2) * 2 * width, 2 * width), 2 * width)
            value = panels_ref[source, :, lanes]
            swapped = jnp.concatenate([value[:, width:], value[:, :width]], axis=1)
            odd = lax.rem(place, 2)
            same = jnp.full(value.shape, lax.rem(slot, 2), jnp.int32) == odd
            value = jnp.where(same, value, swapped)
            mine = (half == (jnp.full(value.shape, odd, jnp.int32) == 1)) & jnp.full(value.shape, real)
            pieces.append((inner, place, jnp.where(mine, value, jnp.zeros_like(value))))
        for inner, place, value in pieces:
            lanes = pl.ds(pl.multiple_of(lax.div(place, 2) * 2 * width, 2 * width), 2 * width)
            lines = pl.ds(pl.multiple_of(inner * width, width), width)
            right_ref[0, lines, lanes] += value
        return carry

    lax.fori_loop(0, lax.div(count_ref[row] + UNROLL - 1, UNROLL), one, 0)
    total = None
    depth = group_size * width
    for group in range(left_ref.shape[0]):
        part = jnp.dot(
            left_ref[group, 0], right_ref[0, group * depth:(group + 1) * depth, :],
            preferred_element_type=jnp.float32,
        )
        total = part if total is None else total + part
    square_ref[0] = total.astype(square_ref.dtype)


def second_kernel(left_ref, right_ref, square_ref, out_ref):
    total = None
    depth = left_ref.shape[3]
    for group in range(left_ref.shape[0]):
        part = jnp.dot(
            left_ref[group, 0], right_ref[0, group * depth:(group + 1) * depth, :],
            preferred_element_type=jnp.float32,
        )
        total = part if total is None else total + part
    out_ref[0] = 3.0 * square_ref[0].astype(jnp.float32) - 2.0 * total


def shards(density, columns):
    rows, width, depth = density.shape
    total, stored = columns.shape
    group_size = depth // width
    groups = stored // group_size
    span = -(-REACH // rows)
    count, codes = live_list(columns, rows, width, group_size, span)
    panels = [
        density if offset == 0 else passed_along(density, "row", -offset)
        for offset in range(-span, span + 1)
    ]
    panels = jnp.concatenate(panels, axis=0)
    left = lax.all_gather(density, "col", axis=0)
    left_spec = pl.BlockSpec((groups, 1, width, depth), lambda i, *_: (0, i, 0, 0))
    right_spec = pl.BlockSpec((1, stored * width, depth), lambda i, *_: (i, 0, 0))
    row_spec = pl.BlockSpec((1, width, depth), lambda i, *_: (i, 0, 0))
    right, square = pl.pallas_call(
        functools.partial(first_kernel, stored, group_size, width),
        grid_spec=pltpu.PrefetchScalarGridSpec(
            num_scalar_prefetch=2,
            grid=(rows,),
            in_specs=[pl.BlockSpec(panels.shape, lambda i, *_: (0, 0, 0)), left_spec],
            out_specs=[right_spec, row_spec],
        ),
        out_shape=[
            jax.ShapeDtypeStruct((rows, stored * width, depth), density.dtype),
            jax.ShapeDtypeStruct(density.shape, density.dtype),
        ],
        compiler_params=pltpu.CompilerParams(vmem_limit_bytes=40 * 1024 * 1024),
    )(count, codes, panels, left)
    gathered = lax.all_gather(square, "col", axis=0)
    return pl.pallas_call(
        second_kernel,
        grid=(rows,),
        in_specs=[left_spec, right_spec, row_spec],
        out_specs=row_spec,
        out_shape=jax.ShapeDtypeStruct(density.shape, jnp.float32),
        compiler_params=pltpu.CompilerParams(vmem_limit_bytes=40 * 1024 * 1024),
    )(gathered, right, square)


def solution(mesh):
    placed = (P("row", None, "col"), P())
    return jax.shard_map(
        shards, mesh=mesh, in_specs=placed, out_specs=P("row", None, "col"), check_vma=False
    )
```

time: 265 us -> 210 us (0.79)
  local copies, waits for them, and re-layouts: 101 us -> 17.1 us
  matrix products: 37.7 us -> 0 us
  Pallas kernels: 0 us -> 36.5 us
  starting transfers between devices: 11.6 us -> 29.4 us
  waiting for transfers between devices: 96.6 us -> 110 us
    dot_general x2 -> x0, matrix products: 37.7 us -> none  [accumulate(): jnp.einsum('ixby,iabyz->ixaz', left, chosen, preferred_element_type=jnp.f...]
    pallas_call x0 -> x2, Pallas kernels: none -> 36.5 us  [the longest x1 22 us: shards(): pl.pallas_call(functools.partial(first_kernel, stored, group_size, width)...]
    gather x3 -> x1, local copies, waits for them, and re-layouts: 32.9 us -> 0.73 us  [live_list(): candidates = jnp.take(group, own, axis=0)]
    another operation x8 -> x0, local copies, waits for them, and re-layouts: 26.3 us -> none  [shards(): stacked = jnp.stack(panels)]
    ppermute x6, starting transfers between devices: 11.5 us -> 29.4 us  [passed_along(): return lax.ppermute(block, axis, route)]
    ppermute x6, waiting for transfers between devices: 81.3 us -> 98.3 us  [passed_along(): return lax.ppermute(block, axis, route)]
    reshape x2 -> x1, local copies, waits for them, and re-layouts: 12.7 us -> 0.06 us  [live_list(): flat = live.reshape(rows, stored * group_size)]
    mul x3 -> x0, local copies, waits for them, and re-layouts: 8.82 us -> none  [the longest x2 8.75 us: shards(): return 3.0 * square.astype(jnp.float32) - 2.0 * cube]
  transfers between devices with their start and end apart: 8 -> 8, of which waited for: 3 -> 3; matrix products, arithmetic and copies ran while one was open for 30% -> 5% of each run, Pallas kernels for 0% -> 0%
where the time goes in v1:
time: 210 us
  waiting for transfers between devices  110 us (52%)
  Pallas kernels  36.5 us (17%)
  starting transfers between devices  29.4 us (14%)
  local copies, waits for them, and re-layouts  17.1 us (8%)
  between operations  13.6 us (6%)
  other arithmetic  3 us (1%)
    ppermute x6, waiting for transfers between devices, passed_along(): return lax.ppermute(block, axis, route)  98.3 us
    ppermute x6, starting transfers between devices, passed_along(): return lax.ppermute(block, axis, route)  29.4 us
    pallas_call x1, Pallas kernels, shards(): pl.pallas_call(functools.partial(first_kernel, stored, group_size, width)...  22 us
    pallas_call x1, Pallas kernels, shards(): pl.pallas_call(second_kernel, grid=(rows,), in_specs=[left_spec, right_sp...  14.5 us
    unnamed x17, local copies, waits for them, and re-layouts  13.6 us
    all_gather x1, waiting for transfers between devices, shards(): gathered = lax.all_gather(square, 'col', axis=0)  10.9 us
  transfers between devices with their start and end apart: 8, of which 3 were waited for; matrix products, arithmetic and copies ran while one was open for 5% of the time, Pallas kernels for 0%

profile of v1, /device:TPU:0, one launch (start us, length us, event | category | flops | bytes accessed | tf_op | source)
XLA Modules:
  0.0 209.6 jit_solution(10286889531116282842)
XLA Ops:
  6.5 0.0 copy-start.4
  6.5 0.0 all-gather.5.cloned.1.call-start
  6.5 0.7 all-gather.5.cloned.1.call-update
  7.3 0.0 all-gather.7.cloned.1.call-start
  7.3 6.1 %collective-permute-start.4 = (bf16[16,64,512]{2,1,0:T(8,128)(2,1)}, bf16[16,64,512]{2,1,0:T(8,128)(2,1)S(1)}, u32[]{:S(2)}, u32[]{:S(2)}) collective-permute-start(bf16[16,64,512]{2,1,0:T(8,128)(2,1)} %param.2), channel_id=1, source_target_pairs={{4,0},{6,2},{8,4},{10,6},{12,8},{14,10},{16,12},{18,14},{20,16},{2... | collective-permute-start | bytes 3145736 | tf_op jit(solution)/shard_map/ppermute | solution.py:17
  13.4 1.4 collective-permute-start.3
  14.8 0.6 collective-permute-start.2
  15.4 0.9 collective-permute-start.1
  16.3 0.8 collective-permute-start
  17.1 0.7 constant_dynamic-slice_fusion
  17.8 0.8 fusion.2
  18.6 0.8 compare_and_fusion
  19.4 0.8 dynamic_slice.11
  20.2 0.1 copy.35
  20.3 0.1 add.116
  20.4 0.1 add.112
  20.4 0.1 copy.31
  20.5 0.1 copy.33
  20.6 0.1 reshape.69
  20.7 0.1 copy.39
  20.8 0.1 copy.42
  20.9 0.7 gather_fusion
  21.6 0.1 broadcast_select_fusion
  21.8 0.1 copy.34
  21.8 0.3 compare_reduce_fusion
  22.1 0.1 copy.36
  22.2 0.2 fusion
  22.5 0.1 copy.40
  22.6 0.1 copy.41
  22.7 0.1 copy.38
  22.7 0.1 copy.37
  22.8 0.3 reduce_window_sum.11
  23.1 0.2 slice_reduce_fusion.count_ref
  23.3 0.5 select_reduce_fusion
  23.8 58.8 %collective-permute-done = bf16[16,64,512]{2,1,0:T(8,128)(2,1)} collective-permute-done((bf16[16,64,512]{2,1,0:T(8,128)(2,1)}, bf16[16,64,512]{2,1,0:T(8,128)(2,1)}, u32[]{:S(2)}, u32[]{:S(2)}) %collective-permute-start) | collective-permute-done | bytes 1048608 | tf_op jit(solution)/shard_map/ppermute | solution.py:17
  82.6 19.6 %collective-permute-start.5 = (bf16[16,64,512]{2,1,0:T(8,128)(2,1)}, bf16[16,64,512]{2,1,0:T(8,128)(2,1)S(1)}, u32[]{:S(2)}, u32[]{:S(2)}) collective-permute-start(bf16[16,64,512]{2,1,0:T(8,128)(2,1)} %param.2), channel_id=1, source_target_pairs={{6,0},{8,2},{10,4},{12,6},{14,8},{16,10},{18,12},{20,14},{22,16},{... | collective-permute-start | bytes 3145736 | tf_op jit(solution)/shard_map/ppermute | solution.py:17
  102.1 1.3 constant_dynamic-update-slice_fusion.6
  103.5 0.0 collective-permute-done.1
  103.5 1.3 constant_dynamic-update-slice_fusion.5
  104.8 0.0 collective-permute-done.2
  104.8 1.3 constant_dynamic-update-slice_fusion.4
  106.1 0.0 copy-done.4
  106.1 0.1 constant_dynamic-update-slice_fusion.3
  106.2 0.0 collective-permute-done.3
  106.3 0.1 constant_dynamic-update-slice_fusion.2
  106.4 0.0 collective-permute-done.4
  106.4 0.1 constant_dynamic-update-slice_fusion.1
  106.5 39.5 %collective-permute-done.5 = bf16[16,64,512]{2,1,0:T(8,128)(2,1)S(1)} collective-permute-done((bf16[16,64,512]{2,1,0:T(8,128)(2,1)}, bf16[16,64,512]{2,1,0:T(8,128)(2,1)S(1)}, u32[]{:S(2)}, u32[]{:S(2)}) %collective-permute-start.5) | collective-permute-done | bytes 1048608 | tf_op jit(solution)/shard_map/ppermute | solution.py:17
  146.0 0.1 constant_dynamic-update-slice_fusion.panels_ref
  146.1 0.0 copy-start
  146.1 2.9 %copy-done = bf16[112,64,512]{2,1,0:T(8,128)(2,1)} copy-done((bf16[112,64,512]{2,1,0:T(8,128)(2,1)}, bf16[112,64,512]{2,1,0:T(8,128)(2,1)S(1)}, u32[]{:S(2)}) %copy-start) | copy-done | bytes 7340056
  149.0 0.0 all-gather.5.cloned.1.call-done
  149.0 0.0 copy-start.1
  149.0 3.1 %copy-done.1 = bf16[112,64,512]{2,1,0:T(8,128)(2,1)S(1)} copy-done((bf16[112,64,512]{2,1,0:T(8,128)(2,1)S(1)}, bf16[112,64,512]{2,1,0:T(8,128)(2,1)}, u32[]{:S(2)}) %copy-start.1) | copy-done | bytes 7340056
  152.1 0.0 copy-start.2
  152.1 1.6 copy-done.2
  153.7 22.0 %shard_map.28 = (bf16[16,1024,512]{2,1,0:T(8,128)(2,1)}, bf16[16,64,512]{2,1,0:T(8,128)(2,1)}) custom-call(s32[16]{0:T(128)S(1)} %slice_reduce_fusion.count_ref, s32[16,128]{1,0:T(8,128)S(1)} %broadcast_add_fusion.code_ref, bf16[112,64,512]{2,1,0:T(8,128)(2,1)S(1)} %copy-done.1, bf16[2,16,64,512]{3,2,1,0:T(8,128)(2,1)S(1)} %bitcast.8), custom_call_target="tpu_custom_call" | custom-call | tf_op jit(solution)/shard_map/pallas_call | solution.py:115
  175.7 0.0 all-gather.7.cloned.1.call-update
  175.7 10.9 %all-gather.7.cloned.1.call-done = bf16[32,64,512]{2,1,0:T(8,128)(2,1)} async-done(((bf16[16,64,512]{2,1,0:T(8,128)(2,1)}), bf16[32,64,512]{2,1,0:T(8,128)(2,1)}) %all-gather.7.cloned.1.call-update) | async-done | bytes 2097168 | tf_op jit(solution)/shard_map/all_gather | solution.py:129
  186.6 0.0 copy-start.3
  186.6 1.6 copy-done.3
  188.2 14.5 %shard_map.29 = f32[16,64,512]{2,1,0:T(8,128)} custom-call(bf16[2,16,64,512]{3,2,1,0:T(8,128)(2,1)S(1)} %bitcast.9, bf16[16,1024,512]{2,1,0:T(8,128)(2,1)} %get-tuple-element.8.right_ref, bf16[16,64,512]{2,1,0:T(8,128)(2,1)} %get-tuple-element.7.square_ref), custom_call_target="tpu_custom_call" | custom-call | tf_op jit(solution)/shard_map/pallas_call | solution.py:130
  (8 shorter events, 0.1 us)
Async XLA Ops:
  6.5 99.6 %copy-start.4 = (bf16[16,64,512]{2,1,0:T(8,128)(2,1)S(1)}, bf16[16,64,512]{2,1,0:T(8,128)(2,1)}, u32[]{:S(2)}) copy-start(bf16[16,64,512]{2,1,0:T(8,128)(2,1)} %param.2) | copy-start | bytes 3145732
  6.5 142.5 %all-gather.5.cloned.1.call-start = ((), (), s32[]{:S(2)}) async-start(), calls=%async_computation | async-start | bytes 3145728 | tf_op jit(solution)/shard_map/all_gather | solution.py:111
  7.3 179.4 %all-gather.7.cloned.1.call-start = ((), (), s32[]{:S(2)}) async-start(), calls=%async_computation.1 | async-start | bytes 3145728 | tf_op jit(solution)/shard_map/all_gather | solution.py:129
  7.3 99.0 %collective-permute-start.4 = (bf16[16,64,512]{2,1,0:T(8,128)(2,1)}, bf16[16,64,512]{2,1,0:T(8,128)(2,1)S(1)}, u32[]{:S(2)}, u32[]{:S(2)}) collective-permute-start(bf16[16,64,512]{2,1,0:T(8,128)(2,1)} %param.2), channel_id=1, source_target_pairs={{4,0},{6,2},{8,4},{10,6},{12,8},{14,10},{16,12},{18,14},{20,16},{2... | collective-permute-start | bytes 3145736 | tf_op jit(solution)/shard_map/ppermute | solution.py:17
  13.4 92.9 %collective-permute-start.3 = (bf16[16,64,512]{2,1,0:T(8,128)(2,1)}, bf16[16,64,512]{2,1,0:T(8,128)(2,1)S(1)}, u32[]{:S(2)}, u32[]{:S(2)}) collective-permute-start(bf16[16,64,512]{2,1,0:T(8,128)(2,1)} %param.2), channel_id=1, source_target_pairs={{2,0},{4,2},{6,4},{8,6},{10,8},{12,10},{14,12},{16,14},{18,16},{20... | collective-permute-start | bytes 3145736 | tf_op jit(solution)/shard_map/ppermute | solution.py:17
  14.8 90.0 %collective-permute-start.2 = (bf16[16,64,512]{2,1,0:T(8,128)(2,1)}, bf16[16,64,512]{2,1,0:T(8,128)(2,1)}, u32[]{:S(2)}, u32[]{:S(2)}) collective-permute-start(bf16[16,64,512]{2,1,0:T(8,128)(2,1)} %param.2), channel_id=1, source_target_pairs={{30,0},{0,2},{2,4},{4,6},{6,8},{8,10},{10,12},{12,14},{14,16},{16,... | collective-permute-start | bytes 3145736 | tf_op jit(solution)/shard_map/ppermute | solution.py:17
  15.4 88.1 %collective-permute-start.1 = (bf16[16,64,512]{2,1,0:T(8,128)(2,1)}, bf16[16,64,512]{2,1,0:T(8,128)(2,1)}, u32[]{:S(2)}, u32[]{:S(2)}) collective-permute-start(bf16[16,64,512]{2,1,0:T(8,128)(2,1)} %param.2), channel_id=1, source_target_pairs={{28,0},{30,2},{0,4},{2,6},{4,8},{6,10},{8,12},{10,14},{12,16},{14,... | collective-permute-start | bytes 3145736 | tf_op jit(solution)/shard_map/ppermute | solution.py:17
  16.3 66.2 %collective-permute-start = (bf16[16,64,512]{2,1,0:T(8,128)(2,1)}, bf16[16,64,512]{2,1,0:T(8,128)(2,1)}, u32[]{:S(2)}, u32[]{:S(2)}) collective-permute-start(bf16[16,64,512]{2,1,0:T(8,128)(2,1)} %param.2), channel_id=1, source_target_pairs={{26,0},{28,2},{30,4},{0,6},{2,8},{4,10},{6,12},{8,14},{10,16},{12,... | collective-permute-start | bytes 3145736 | tf_op jit(solution)/shard_map/ppermute | solution.py:17
  82.6 63.4 %collective-permute-start.5 = (bf16[16,64,512]{2,1,0:T(8,128)(2,1)}, bf16[16,64,512]{2,1,0:T(8,128)(2,1)S(1)}, u32[]{:S(2)}, u32[]{:S(2)}) collective-permute-start(bf16[16,64,512]{2,1,0:T(8,128)(2,1)} %param.2), channel_id=1, source_target_pairs={{6,0},{8,2},{10,4},{12,6},{14,8},{16,10},{18,12},{20,14},{22,16},{... | collective-permute-start | bytes 3145736 | tf_op jit(solution)/shard_map/ppermute | solution.py:17
  146.1 2.9 %copy-start = (bf16[112,64,512]{2,1,0:T(8,128)(2,1)}, bf16[112,64,512]{2,1,0:T(8,128)(2,1)S(1)}, u32[]{:S(2)}) copy-start(bf16[112,64,512]{2,1,0:T(8,128)(2,1)S(1)} %constant_dynamic-update-slice_fusion.panels_ref) | copy-start | bytes 22020100
  149.0 3.1 %copy-start.1 = (bf16[112,64,512]{2,1,0:T(8,128)(2,1)S(1)}, bf16[112,64,512]{2,1,0:T(8,128)(2,1)}, u32[]{:S(2)}) copy-start(bf16[112,64,512]{2,1,0:T(8,128)(2,1)} %copy-done) | copy-start | bytes 22020100
  152.1 1.6 copy-start.2
  186.6 1.6 copy-start.3
Sparse Core Ops, SparseCore 0:
  8.9 13.2 all-gather.4
  175.8 10.7 all-gather.6

commit v2 on v1

--- a/solution.py
+++ b/solution.py
@@ -11,10 +11,160 @@
 UNROLL = 4
 
 
-def passed_along(block, axis, distance):
-    size = lax.axis_size(axis)
-    route = [((i - distance) % size, i) for i in range(size)]
-    return lax.ppermute(block, axis, route)
+def greet(devices):
+    barrier = pltpu.get_barrier_semaphore()
+    for device in devices:
+        pl.semaphore_signal(barrier, inc=1, device_id=device, device_id_type=pl.DeviceIdType.MESH)
+    pl.semaphore_wait(barrier, len(devices))
+
+
+def col_peers(groups):
+    return [{"col": lax.rem(lax.axis_index("col") + step, groups)} for step in range(1, groups)]
+
+
+def share_with_peers(groups, block, shared, local_sem, send_sem, recv_sem):
+    here = lax.axis_index("col")
+    local = pltpu.make_async_copy(block, shared.at[here], local_sem)
+    local.start()
+    copies = []
+    for step, peer in enumerate(col_peers(groups)):
+        copies.append(pltpu.make_async_remote_copy(
+            src_ref=block, dst_ref=shared.at[here], send_sem=send_sem.at[step], recv_sem=recv_sem.at[step],
+            device_id=peer, device_id_type=pl.DeviceIdType.MESH,
+        ))
+        copies[-1].start()
+    return local, copies
+
+
+def exchange_kernel(groups, block, shared, local_sem, send_sem, recv_sem):
+    greet(col_peers(groups))
+    local, copies = share_with_peers(groups, block, shared, local_sem, send_sem, recv_sem)
+    for copy in copies:
+        copy.wait()
+    local.wait()
+
+
+def exchange(block, groups, collective_id):
+    return pl.pallas_call(
+        functools.partial(exchange_kernel, groups),
+        in_specs=[pl.BlockSpec(memory_space=pl.ANY)],
+        out_specs=pl.BlockSpec(memory_space=pl.ANY),
+        out_shape=jax.ShapeDtypeStruct((groups,) + block.shape, block.dtype),
+        scratch_shapes=[
+            pltpu.SemaphoreType.DMA,
+            pltpu.SemaphoreType.DMA((groups - 1,)),
+            pltpu.SemaphoreType.DMA((groups - 1,)),
+        ],
+        compiler_params=pltpu.CompilerParams(collective_id=collective_id, has_side_effects=True),
+    )(block)
+
+
+def direct_kernel(groups, size, span, block, panels, shared, own_sem, local_sem, col_send, col_recv, send_sem, recv_sem):
+    me = lax.axis_index("row")
+    offsets = [d for d in range(-span, span + 1) if d != 0]
+    greet([{"row": lax.rem(me + d + size, size)} for d in offsets] + col_peers(groups))
+    own = pltpu.make_async_copy(block, panels.at[span], own_sem)
+    own.start()
+    local, copies = share_with_peers(groups, block, shared, local_sem, col_send, col_recv)
+    for step, d in enumerate(offsets):
+        copies.append(pltpu.make_async_remote_copy(
+            src_ref=block, dst_ref=panels.at[span - d], send_sem=send_sem.at[step], recv_sem=recv_sem.at[step],
+            device_id={"row": lax.rem(me + d + size, size)}, device_id_type=pl.DeviceIdType.MESH,
+        ))
+        copies[-1].start()
+    for copy in copies:
+        copy.wait()
+    local.wait()
+    own.wait()
+
+
+def relay_kernel(groups, size, chunks, block, panels, shared, own_sem, local_sem, col_send, col_recv, send_sem, recv_sem):
+    me = lax.axis_index("row")
+    x_step = 1 - 2 * lax.rem(me, 2)
+    y_step = 2 - 4 * lax.rem(lax.div(me, 2), 2)
+    steps = [x_step, y_step, x_step + y_step]
+    x_near, y_near = me + x_step, me + y_step
+    above, below = lax.rem(me + 4, size), lax.rem(me + size - 4, size)
+    greet([{"row": d} for d in (x_near, y_near, above, below)] + col_peers(groups))
+    own = pltpu.make_async_copy(block, panels.at[3], own_sem)
+    own.start()
+    local, others = share_with_peers(groups, block, shared, local_sem, col_send, col_recv)
+    depth = block.shape[0] // chunks
+
+    def send(kind, chunk, source, slot, device):
+        lines = pl.ds(chunk * depth, depth)
+        copy = pltpu.make_async_remote_copy(
+            src_ref=source.at[lines], dst_ref=panels.at[slot, lines],
+            send_sem=send_sem.at[kind, chunk], recv_sem=recv_sem.at[kind, chunk],
+            device_id={"row": device}, device_id_type=pl.DeviceIdType.MESH,
+        )
+        copy.start()
+        others.append(copy)
+        return copy
+
+    def pass_on(kind, chunk):
+        step = steps[kind]
+        sign = jnp.where(step > 0, 1, -1)
+        target = lax.rem(me + 4 * sign + size, size)
+        late.append(send(3 + kind, chunk, panels.at[3 + step], 3 + step - 4 * sign, target))
+
+    late, arriving = [], []
+    for chunk in range(chunks):
+        arriving.append((
+            send(0, chunk, block, 3 - x_step, x_near),
+            send(1, chunk, block, 3 - y_step, y_near),
+        ))
+    corner = []
+    lag = 2
+    for chunk in range(chunks + lag):
+        if chunk < chunks:
+            arriving[chunk][0].wait_recv()
+            if chunk % 2 == 0:
+                corner.append(send(2, chunk, panels.at[3 + x_step], 3 + x_step - y_step, y_near))
+            pass_on(0, chunk)
+            arriving[chunk][1].wait_recv()
+            if chunk % 2 == 1:
+                corner.append(send(2, chunk, panels.at[3 + y_step], 3 + y_step - x_step, x_near))
+            pass_on(1, chunk)
+        if chunk >= lag:
+            corner[chunk - lag].wait_recv()
+            pass_on(2, chunk - lag)
+    for copy in late:
+        copy.wait_recv()
+    for copy in others[:groups - 1]:
+        copy.wait_recv()
+    for copy in others:
+        copy.wait_send()
+    local.wait()
+    own.wait()
+
+
+def fetch(density, groups, size, span, planes):
+    chunks = 8
+    if planes:
+        body, shape = functools.partial(relay_kernel, groups, size, chunks), (6, chunks)
+    else:
+        body, shape = functools.partial(direct_kernel, groups, size, span), (2 * span,)
+    anywhere = pl.BlockSpec(memory_space=pl.ANY)
+    panels, shared = pl.pallas_call(
+        body,
+        in_specs=[anywhere],
+        out_specs=[anywhere, anywhere],
+        out_shape=[
+            jax.ShapeDtypeStruct((2 * span + 1,) + density.shape, density.dtype),
+            jax.ShapeDtypeStruct((groups,) + density.shape, density.dtype),
+        ],
+        scratch_shapes=[
+            pltpu.SemaphoreType.DMA,
+            pltpu.SemaphoreType.DMA,
+            pltpu.SemaphoreType.DMA((groups - 1,)),
+            pltpu.SemaphoreType.DMA((groups - 1,)),
+            pltpu.SemaphoreType.DMA(shape),
+            pltpu.SemaphoreType.DMA(shape),
+        ],
+        compiler_params=pltpu.CompilerParams(collective_id=0, has_side_effects=True),
+    )(density)
+    return panels.reshape((-1,) + density.shape[1:]), shared
 
 
 def live_list(columns, rows, width, group_size, span):
@@ -103,12 +253,9 @@
     groups = stored // group_size
     span = -(-REACH // rows)
     count, codes = live_list(columns, rows, width, group_size, span)
-    panels = [
-        density if offset == 0 else passed_along(density, "row", -offset)
-        for offset in range(-span, span + 1)
-    ]
-    panels = jnp.concatenate(panels, axis=0)
-    left = lax.all_gather(density, "col", axis=0)
+    size = lax.axis_size("row")
+    planes = (size, groups, span) == (16, 2, 3)
+    panels, left = fetch(density, groups, size, span, planes)
     left_spec = pl.BlockSpec((groups, 1, width, depth), lambda i, *_: (0, i, 0, 0))
     right_spec = pl.BlockSpec((1, stored * width, depth), lambda i, *_: (i, 0, 0))
     row_spec = pl.BlockSpec((1, width, depth), lambda i, *_: (i, 0, 0))
@@ -126,7 +273,7 @@
         ],
         compiler_params=pltpu.CompilerParams(vmem_limit_bytes=40 * 1024 * 1024),
     )(count, codes, panels, left)
-    gathered = lax.all_gather(square, "col", axis=0)
+    gathered = exchange(square, groups, 1)
     return pl.pallas_call(
         second_kernel,
         grid=(rows,),

time: 210 us -> 170 us (0.81)
  Pallas kernels: 36.5 us -> 156 us
  waiting for transfers between devices: 110 us -> 0 us
  starting transfers between devices: 29.4 us -> 0 us
  between operations: 13.6 us -> 0.15 us
  local copies, waits for them, and re-layouts: 17.1 us -> 10.8 us
    pallas_call x0 -> x2, Pallas kernels: none -> 119 us  [the longest x1 85.7 us: fetch(): pl.pallas_call(body, in_specs=[anywhere], out_specs=[anywhere, anywhere],...]
    ppermute x6 -> x0, waiting for transfers between devices: 98.3 us -> none  [passed_along(): return lax.ppermute(block, axis, route)]
    ppermute x6 -> x0, starting transfers between devices: 29.4 us -> none  [passed_along(): return lax.ppermute(block, axis, route)]
    all_gather x2 -> x0, waiting for transfers between devices: 10.9 us -> none  [the longest x1 10.9 us: shards(): gathered = lax.all_gather(square, 'col', axis=0)]
    unnamed x17 -> x11, local copies, waits for them, and re-layouts: 13.6 us -> 7.37 us
  transfers between devices with their start and end apart: 8 -> 0, of which waited for: 3 -> 0; matrix products, arithmetic and copies ran while one was open for 5% -> 0% of each run, Pallas kernels for 0% -> 0%
where the time goes in v2:
time: 170 us
  Pallas kernels  156 us (92%)
  local copies, waits for them, and re-layouts  10.8 us (6%)
  other arithmetic  2.99 us (2%)
    pallas_call x1, Pallas kernels, fetch(): pl.pallas_call(body, in_specs=[anywhere], out_specs=[anywhere, anywhere],...  85.7 us
    pallas_call x1, Pallas kernels, exchange(): pl.pallas_call(functools.partial(exchange_kernel, groups), in_specs=[pl.B...  32.9 us
    pallas_call x1, Pallas kernels, shards(): pl.pallas_call(functools.partial(first_kernel, stored, group_size, width)...  22.5 us
    pallas_call x1, Pallas kernels, shards(): pl.pallas_call(second_kernel, grid=(rows,), in_specs=[left_spec, right_sp...  14.5 us
    unnamed x11, local copies, waits for them, and re-layouts  7.37 us

profile of v2, /device:TPU:0, one launch (start us, length us, event | category | flops | bytes accessed | tf_op | source)
XLA Modules:
  0.0 169.5 jit_solution(12099922289092210464)
XLA Ops:
  0.0 0.8 dynamic_slice.11
  0.8 0.1 copy.28
  0.9 0.8 fusion.2
  1.6 0.7 constant_dynamic-slice_fusion
  2.4 0.1 add.116
  2.5 0.1 add.112
  2.5 0.8 compare_and_fusion
  3.3 0.1 copy.24
  3.4 0.1 copy.26
  3.5 0.1 reshape.73
  3.6 0.1 copy.32
  3.6 0.1 copy.35
  3.8 0.7 gather_fusion
  4.5 0.1 broadcast_select_fusion
  4.6 0.1 copy.27
  4.7 0.3 compare_reduce_fusion
  5.0 0.2 fusion
  5.2 0.1 copy.29
  5.3 0.1 copy.33
  5.5 0.1 copy.34
  5.5 0.1 copy.31
  5.6 0.1 copy.30
  5.7 0.3 reduce_window_sum.11
  6.0 0.5 select_reduce_fusion
  6.5 0.2 slice_reduce_fusion.count_ref
  6.6 85.7 %shard_map.28 = (bf16[7,16,64,512]{3,2,1,0:T(8,128)(2,1)}, bf16[2,16,64,512]{3,2,1,0:T(8,128)(2,1)}) custom-call(bf16[16,64,512]{2,1,0:T(8,128)(2,1)} %block.1), custom_call_target="tpu_custom_call" | custom-call | tf_op jit(solution)/shard_map/pallas_call | solution.py:149
  92.4 0.0 copy-start.1
  92.4 3.1 %copy-done.1 = bf16[7,16,64,512]{3,2,1,0:T(8,128)(2,1)S(1)} copy-done((bf16[7,16,64,512]{3,2,1,0:T(8,128)(2,1)S(1)}, bf16[7,16,64,512]{3,2,1,0:T(8,128)(2,1)}, u32[]{:S(2)}) %copy-start.1) | copy-done | bytes 7340056
  95.5 0.0 copy-start.4
  95.5 1.6 copy-done.4
  97.1 22.5 %shard_map.29 = (bf16[16,1024,512]{2,1,0:T(8,128)(2,1)}, bf16[16,64,512]{2,1,0:T(8,128)(2,1)S(1)}) custom-call(s32[16]{0:T(128)S(1)} %slice_reduce_fusion.count_ref, s32[16,128]{1,0:T(8,128)S(1)} %broadcast_add_fusion.code_ref, bf16[112,64,512]{2,1,0:T(8,128)(2,1)S(1)} %bitcast.7, bf16[2,16,64,512]{3,2,1,0:T(8,128)(2,1)S(1)} %copy-done.4), custom_call_target="tpu_custom_call" | custom-call | tf_op jit(solution)/shard_map/pallas_call | solution.py:262
  119.6 0.0 copy-start.2
  119.6 1.0 copy-done.2
  120.6 0.0 copy-start.3
  120.6 32.9 %shard_map.30.left_ref = bf16[2,16,64,512]{3,2,1,0:T(8,128)(2,1)} custom-call(bf16[16,64,512]{2,1,0:T(8,128)(2,1)} %copy-done.2), custom_call_target="tpu_custom_call" | custom-call | tf_op jit(solution)/shard_map/pallas_call | solution.py:48
  153.5 0.0 copy-done.3
  153.5 0.0 copy-start
  153.5 1.6 copy-done
  155.1 14.5 %shard_map.31 = f32[16,64,512]{2,1,0:T(8,128)} custom-call(bf16[2,16,64,512]{3,2,1,0:T(8,128)(2,1)S(1)} %copy-done, bf16[16,1024,512]{2,1,0:T(8,128)(2,1)} %get-tuple-element.12.right_ref, bf16[16,64,512]{2,1,0:T(8,128)(2,1)S(1)} %copy-done.3), custom_call_target="tpu_custom_call" | custom-call | tf_op jit(solution)/shard_map/pallas_call | solution.py:277
  (8 shorter events, 0.1 us)
Async XLA Ops:
  92.4 3.1 %copy-start.1 = (bf16[7,16,64,512]{3,2,1,0:T(8,128)(2,1)S(1)}, bf16[7,16,64,512]{3,2,1,0:T(8,128)(2,1)}, u32[]{:S(2)}) copy-start(bf16[7,16,64,512]{3,2,1,0:T(8,128)(2,1)} %get-tuple-element.9) | copy-start | bytes 22020100
  95.5 1.6 copy-start.4
  119.6 1.0 copy-start.2
  120.6 32.9 %copy-start.3 = (bf16[16,64,512]{2,1,0:T(8,128)(2,1)S(1)}, bf16[16,64,512]{2,1,0:T(8,128)(2,1)}, u32[]{:S(2)}) copy-start(bf16[16,64,512]{2,1,0:T(8,128)(2,1)} %copy-done.2) | copy-start | bytes 3145732
  153.5 1.6 copy-start

commit v3 on v2

v3 whole, which is shorter than its diff:
```python
import functools

import jax
import jax.numpy as jnp
from jax import lax
from jax.experimental import pallas as pl
from jax.experimental.pallas import tpu as pltpu
from jax.sharding import PartitionSpec as P

REACH = 48
UNROLL = 4
PIECES = 8


def greet(devices):
    barrier = pltpu.get_barrier_semaphore()
    for device in devices:
        pl.semaphore_signal(barrier, inc=1, device_id=device, device_id_type=pl.DeviceIdType.MESH)
    pl.semaphore_wait(barrier, len(devices))


def col_peers(groups):
    return [{"col": lax.rem(lax.axis_index("col") + step, groups)} for step in range(1, groups)]


def share_with_peers(groups, block, shared, send_sem, recv_sem):
    copies = []
    chunks = send_sem.shape[1]
    depth = block.shape[0] // chunks
    for step, peer in enumerate(col_peers(groups)):
        for chunk in range(chunks):
            lines = pl.ds(chunk * depth, depth)
            copies.append(pltpu.make_async_remote_copy(
                src_ref=block.at[lines], dst_ref=shared.at[groups - 2 - step, lines],
                send_sem=send_sem.at[step, chunk], recv_sem=recv_sem.at[step, chunk],
                device_id=peer, device_id_type=pl.DeviceIdType.MESH,
            ))
            copies[-1].start()
    return copies


def exchange_kernel(groups, block, shared, send_sem, recv_sem):
    greet(col_peers(groups))
    for copy in share_with_peers(groups, block, shared, send_sem, recv_sem):
        copy.wait()


def exchange(block, groups, collective_id):
    return pl.pallas_call(
        functools.partial(exchange_kernel, groups),
        in_specs=[pl.BlockSpec(memory_space=pl.ANY)],
        out_specs=pl.BlockSpec(memory_space=pl.ANY),
        out_shape=jax.ShapeDtypeStruct((groups - 1,) + block.shape, block.dtype),
        scratch_shapes=[pltpu.SemaphoreType.DMA((groups - 1, PIECES))] * 2,
        compiler_params=pltpu.CompilerParams(collective_id=collective_id, has_side_effects=True),
    )(block)


def turn(block, turned, pair):
    wide = jnp.concatenate([block[2 * pair], block[2 * pair + 1]], axis=0)
    turned[pair] = wide.T


def direct_kernel(groups, size, span, block, panels, shared, turned, own_sem, col_send, col_recv, send_sem, recv_sem):
    me = lax.axis_index("row")
    offsets = [d for d in range(-span, span + 1) if d != 0]
    greet([{"row": lax.rem(me + d + size, size)} for d in offsets] + col_peers(groups))
    copies = share_with_peers(groups, block, shared, col_send, col_recv)
    for pair in range(turned.shape[0]):
        turn(block, turned, pair)
    own = pltpu.make_async_copy(turned, panels.at[span], own_sem)
    own.start()
    for step, d in enumerate(offsets):
        copies.append(pltpu.make_async_remote_copy(
            src_ref=turned, dst_ref=panels.at[span - d], send_sem=send_sem.at[step], recv_sem=recv_sem.at[step],
            device_id={"row": lax.rem(me + d + size, size)}, device_id_type=pl.DeviceIdType.MESH,
        ))
        copies[-1].start()
    for copy in copies:
        copy.wait()
    own.wait()


def relay_kernel(groups, size, chunks, block, panels, shared, turned, own_sem, col_send, col_recv, send_sem, recv_sem):
    me = lax.axis_index("row")
    x_step = 1 - 2 * lax.rem(me, 2)
    y_step = 2 - 4 * lax.rem(lax.div(me, 2), 2)
    steps = [x_step, y_step, x_step + y_step]
    x_near, y_near = me + x_step, me + y_step
    above, below = lax.rem(me + 4, size), lax.rem(me + size - 4, size)
    greet([{"row": d} for d in (x_near, y_near, above, below)] + col_peers(groups))
    others = []
    depth = turned.shape[0] // chunks

    def send(kind, chunk, source, slot, device):
        lines = pl.ds(chunk * depth, depth)
        copy = pltpu.make_async_remote_copy(
            src_ref=source.at[lines], dst_ref=panels.at[slot, lines],
            send_sem=send_sem.at[kind, chunk], recv_sem=recv_sem.at[kind, chunk],
            device_id={"row": device}, device_id_type=pl.DeviceIdType.MESH,
        )
        copy.start()
        others.append(copy)
        return copy

    def pass_on(kind, chunk):
        step = steps[kind]
        sign = jnp.where(step > 0, 1, -1)
        target = lax.rem(me + 4 * sign + size, size)
        late.append(send(3 + kind, chunk, panels.at[3 + step], 3 + step - 4 * sign, target))

    late, arriving = [], []
    for chunk in range(chunks):
        for pair in range(chunk * depth, (chunk + 1) * depth):
            turn(block, turned, pair)
        arriving.append((
            send(0, chunk, turned, 3 - x_step, x_near),
            send(1, chunk, turned, 3 - y_step, y_near),
        ))
    own = pltpu.make_async_copy(turned, panels.at[3], own_sem)
    own.start()
    col_copies = share_with_peers(groups, block, shared, col_send, col_recv)
    corner = []
    lag = 2
    for chunk in range(chunks + lag):
        if chunk < chunks:
            arriving[chunk][0].wait_recv()
            if chunk % 2 == 0:
                corner.append(send(2, chunk, panels.at[3 + x_step], 3 + x_step - y_step, y_near))
            pass_on(0, chunk)
            arriving[chunk][1].wait_recv()
            if chunk % 2 == 1:
                corner.append(send(2, chunk, panels.at[3 + y_step], 3 + y_step - x_step, x_near))
            pass_on(1, chunk)
        if chunk >= lag:
            corner[chunk - lag].wait_recv()
            pass_on(2, chunk - lag)
    for copy in late:
        copy.wait_recv()
    for copy in others:
        copy.wait_send()
    for copy in col_copies:
        copy.wait()
    own.wait()


def fetch(density, groups, size, span, planes):
    chunks = 8
    if planes:
        body, shape = functools.partial(relay_kernel, groups, size, chunks), (6, chunks)
    else:
        body, shape = functools.partial(direct_kernel, groups, size, span), (2 * span,)
    anywhere = pl.BlockSpec(memory_space=pl.ANY)
    rows, width, depth = density.shape
    turned = (rows // 2, depth, 2 * width)
    panels, shared = pl.pallas_call(
        body,
        in_specs=[pl.BlockSpec(memory_space=pltpu.VMEM)],
        out_specs=[anywhere, anywhere],
        out_shape=[
            jax.ShapeDtypeStruct((2 * span + 1,) + turned, density.dtype),
            jax.ShapeDtypeStruct((groups - 1,) + density.shape, density.dtype),
        ],
        scratch_shapes=[
            pltpu.VMEM(turned, density.dtype),
            pltpu.SemaphoreType.DMA,
            pltpu.SemaphoreType.DMA((groups - 1, PIECES)),
            pltpu.SemaphoreType.DMA((groups - 1, PIECES)),
            pltpu.SemaphoreType.DMA(shape),
            pltpu.SemaphoreType.DMA(shape),
        ],
        compiler_params=pltpu.CompilerParams(
            collective_id=0, has_side_effects=True, vmem_limit_bytes=32 * 1024 * 1024
        ),
    )(density)
    return panels.reshape((-1,) + turned[1:]), shared


def live_list(columns, rows, width, group_size, span):
    total, stored = columns.shape
    base = lax.axis_index("row") * rows
    first = lax.axis_index("col") * group_size
    own = lax.dynamic_slice_in_dim(columns, base, rows, 0)
    wanted = lax.dynamic_slice_in_dim(own, first, group_size, 1)
    group = lax.dynamic_slice_in_dim(columns, first, group_size, 1)
    candidates = jnp.take(group, own, axis=0)
    distance = jnp.mod(own - base + span * rows, total)
    equal = candidates[:, :, :, None] == wanted[:, None, None, :]
    slots = jnp.arange(group_size, dtype=jnp.int32)
    live = jnp.any(equal, axis=-1)
    place = jnp.sum(jnp.where(equal, slots, 0), axis=-1)
    inner = jnp.mod(jnp.arange(stored, dtype=jnp.int32) - first, stored)[None, :, None]
    code = ((distance[:, :, None] * group_size + slots) * stored + inner) * group_size + place
    flat = live.reshape(rows, stored * group_size)
    code = code.reshape(rows, stored * group_size)
    order = jnp.cumsum(flat.astype(jnp.int32), axis=1)
    ranks = jnp.arange(1, stored * group_size + 1, dtype=jnp.int32)
    chosen = flat[:, None, :] & (order[:, None, :] == ranks[None, :, None])
    packed = jnp.sum(jnp.where(chosen, code[:, None, :] + 1, 0), axis=-1)
    return order[:, -1], packed - 1


def multiply(right_ref, left_refs):
    depth = left_refs[0].shape[-1]
    total, start = None, 0
    for left_ref in left_refs:
        part = lax.dot_general(
            right_ref[0, :, start:start + depth], left_ref[...], (((1,), (1,)), ((), ())),
            preferred_element_type=jnp.float32,
        )
        total = part if total is None else total + part
        start += depth
    return total.T


def left_parts(own_ref, shared_ref):
    return [own_ref.at[0]] + [shared_ref.at[step, 0] for step in range(shared_ref.shape[0])]


def first_kernel(stored, group_size, width, count_ref, code_ref, panels_ref, own_ref, shared_ref, right_ref, square_ref):
    row = pl.program_id(0)
    right_ref[...] = jnp.zeros_like(right_ref)
    half = lax.broadcasted_iota(jnp.int32, (width, 2 * width), 1) >= width

    def one(entry, carry):
        pieces = []
        for part in range(UNROLL):
            raw = code_ref[row, entry * UNROLL + part]
            real = raw >= 0
            code = jnp.maximum(raw, 0)
            place = lax.rem(code, group_size)
            code = lax.div(code, group_size)
            inner = lax.rem(code, stored)
            code = lax.div(code, stored)
            slot = lax.rem(code, group_size)
            source = lax.div(code, group_size)
            value = panels_ref[lax.div(source, 2), pl.ds(pl.multiple_of(slot * width, width), width), :]
            swapped = jnp.concatenate([value[:, width:], value[:, :width]], axis=1)
            odd = lax.rem(inner, 2)
            same = jnp.full(value.shape, lax.rem(source, 2), jnp.int32) == odd
            value = jnp.where(same, value, swapped)
            mine = (half == (jnp.full(value.shape, odd, jnp.int32) == 1)) & jnp.full(value.shape, real)
            pieces.append((inner, place, jnp.where(mine, value, jnp.zeros_like(value))))
        for inner, place, value in pieces:
            lanes = pl.ds(pl.multiple_of(lax.div(inner, 2) * 2 * width, 2 * width), 2 * width)
            lines = pl.ds(pl.multiple_of(place * width, width), width)
            right_ref[0, lines, lanes] += value
        return carry

    lax.fori_loop(0, lax.div(count_ref[row] + UNROLL - 1, UNROLL), one, 0)
    square_ref[0] = multiply(right_ref, left_parts(own_ref, shared_ref)).astype(square_ref.dtype)


def second_kernel(own_ref, shared_ref, right_ref, out_ref):
    total = multiply(right_ref, left_parts(own_ref, shared_ref))
    out_ref[0] = 3.0 * own_ref[0].astype(jnp.float32) - 2.0 * total


def shards(density, columns):
    rows, width, depth = density.shape
    total, stored = columns.shape
    group_size = depth // width
    groups = stored // group_size
    span = -(-REACH // rows)
    count, codes = live_list(columns, rows, width, group_size, span)
    size = lax.axis_size("row")
    planes = (size, groups, span) == (16, 2, 3)
    panels, shared = fetch(density, groups, size, span, planes)
    row_spec = pl.BlockSpec((1, width, depth), lambda i, *_: (i, 0, 0))
    shared_spec = pl.BlockSpec((groups - 1, 1, width, depth), lambda i, *_: (0, i, 0, 0))
    right_spec = pl.BlockSpec((1, depth, stored * width), lambda i, *_: (i, 0, 0))
    right, square = pl.pallas_call(
        functools.partial(first_kernel, stored, group_size, width),
        grid_spec=pltpu.PrefetchScalarGridSpec(
            num_scalar_prefetch=2,
            grid=(rows,),
            in_specs=[pl.BlockSpec(panels.shape, lambda i, *_: (0, 0, 0)), row_spec, shared_spec],
            out_specs=[right_spec, row_spec],
        ),
        out_shape=[
            jax.ShapeDtypeStruct((rows, depth, stored * width), density.dtype),
            jax.ShapeDtypeStruct(density.shape, density.dtype),
        ],
        compiler_params=pltpu.CompilerParams(vmem_limit_bytes=40 * 1024 * 1024),
    )(count, codes, panels, density, shared)
    return pl.pallas_call(
        second_kernel,
        grid=(rows,),
        in_specs=[row_spec, shared_spec, right_spec],
        out_specs=row_spec,
        out_shape=jax.ShapeDtypeStruct(density.shape, jnp.float32),
        compiler_params=pltpu.CompilerParams(vmem_limit_bytes=40 * 1024 * 1024),
    )(square, exchange(square, groups, 1), right)


def solution(mesh):
    placed = (P("row", None, "col"), P())
    return jax.shard_map(
        shards, mesh=mesh, in_specs=placed, out_specs=P("row", None, "col"), check_vma=False
    )
```

time: 170 us -> 142 us (0.84)
  Pallas kernels: 156 us -> 129 us
    pallas_call x1, Pallas kernels: 32.9 us -> 3.14 us  [exchange(): pl.pallas_call(functools.partial(exchange_kernel, groups), in_specs=[pl.B...]
    pallas_call x1, Pallas kernels: 22.5 us -> 25.1 us  [shards(): pl.pallas_call(functools.partial(first_kernel, stored, group_size, width)...]
where the time goes in v3:
time: 142 us
  Pallas kernels  129 us (91%)
  local copies, waits for them, and re-layouts  9.49 us (7%)
  other arithmetic  3.01 us (2%)
    pallas_call x1, Pallas kernels, fetch(): pl.pallas_call(body, in_specs=[pl.BlockSpec(memory_space=pltpu.VMEM)], ou...  85.3 us
    pallas_call x1, Pallas kernels, shards(): pl.pallas_call(functools.partial(first_kernel, stored, group_size, width)...  25.1 us
    pallas_call x1, Pallas kernels, shards(): pl.pallas_call(second_kernel, grid=(rows,), in_specs=[row_spec, shared_sp...  15.8 us
    unnamed x11, local copies, waits for them, and re-layouts  6 us
    pallas_call x1, Pallas kernels, exchange(): pl.pallas_call(functools.partial(exchange_kernel, groups), in_specs=[pl.B...  3.14 us

profile of v3, /device:TPU:0, one launch (start us, length us, event | category | flops | bytes accessed | tf_op | source)
XLA Modules:
  0.0 142.0 jit_solution(12918813512137839349)
XLA Ops:
  0.0 0.8 dynamic_slice.11
  0.8 0.1 copy.28
  0.9 0.1 add.126
  1.0 0.1 add.127
  1.1 0.8 fusion.2
  1.8 0.7 constant_dynamic-slice_fusion
  2.5 0.1 add.122
  2.6 0.8 compare_and_fusion
  3.4 0.1 copy.24
  3.5 0.1 copy.26
  3.6 0.1 reshape.88
  3.7 0.1 copy.32
  3.7 0.1 copy.35
  3.9 0.7 gather_fusion
  4.6 0.1 broadcast_select_fusion
  4.7 0.1 copy.27
  4.8 0.3 compare_reduce_fusion
  5.1 0.2 fusion
  5.3 0.1 copy.29
  5.4 0.1 copy.33
  5.5 0.1 copy.34
  5.6 0.1 copy.31
  5.7 0.1 copy.30
  5.8 0.3 reduce_window_sum.11
  6.1 0.5 select_reduce_fusion
  6.5 0.2 slice_reduce_fusion.count_ref
  6.7 0.0 copy-start.3
  6.7 1.2 copy-done.3
  8.0 85.3 %shard_map.28 = (bf16[7,8,512,128]{3,2,1,0:T(8,128)(2,1)S(1)}, bf16[1,16,64,512]{3,2,1,0:T(8,128)(2,1)S(1)}) custom-call(bf16[16,64,512]{2,1,0:T(8,128)(2,1)S(1)} %copy-done.3), custom_call_target="tpu_custom_call" | custom-call | tf_op jit(solution)/shard_map/pallas_call | solution.py:156
  93.2 0.0 copy-start.4
  93.3 1.2 copy-done.4
  94.5 25.1 %shard_map.29 = (bf16[16,512,1024]{2,1,0:T(8,128)(2,1)}, bf16[16,64,512]{2,1,0:T(8,128)(2,1)S(1)}) custom-call(s32[16]{0:T(128)S(1)} %slice_reduce_fusion.count_ref, s32[16,128]{1,0:T(8,128)S(1)} %broadcast_add_fusion.code_ref, bf16[56,512,128]{2,1,0:T(8,128)(2,1)S(1)} %bitcast.7, bf16[16,64,512]{2,1,0:T(8,128)(2,1)S(1)} %copy-done.4, ...), custom_call_target="tpu_custom_call" | custom-call | tf_op jit(solution)/shard_map/pallas_call | solution.py:272
  119.6 0.0 copy-start
  119.6 1.0 copy-done
  120.6 3.1 %shard_map.30.shared_ref = bf16[1,16,64,512]{3,2,1,0:T(8,128)(2,1)} custom-call(bf16[16,64,512]{2,1,0:T(8,128)(2,1)} %copy-done), custom_call_target="tpu_custom_call" | custom-call | tf_op jit(solution)/shard_map/pallas_call | solution.py:49
  123.7 0.0 copy-start.1
  123.7 1.2 copy-done.1
  124.9 0.0 copy-start.2
  124.9 1.2 copy-done.2
  126.2 15.8 %shard_map.31 = f32[16,64,512]{2,1,0:T(8,128)} custom-call(bf16[16,64,512]{2,1,0:T(8,128)(2,1)S(1)} %copy-done.1, bf16[1,16,64,512]{3,2,1,0:T(8,128)(2,1)S(1)} %copy-done.2, bf16[16,512,1024]{2,1,0:T(8,128)(2,1)} %get-tuple-element.12.right_ref), custom_call_target="tpu_custom_call" | custom-call | tf_op jit(solution)/shard_map/pallas_call | solution.py:286
  (8 shorter events, 0.1 us)
Async XLA Ops:
  6.7 1.2 copy-start.3
  93.2 1.2 copy-start.4
  119.6 1.0 copy-start
  123.7 1.2 copy-start.1
  124.9 1.2 copy-start.2

commit v4 on v3

--- a/solution.py
+++ b/solution.py
@@ -200,12 +200,12 @@
     return order[:, -1], packed - 1
 
 
-def multiply(right_ref, left_refs):
+def multiply(right, left_refs):
     depth = left_refs[0].shape[-1]
     total, start = None, 0
     for left_ref in left_refs:
         part = lax.dot_general(
-            right_ref[0, :, start:start + depth], left_ref[...], (((1,), (1,)), ((), ())),
+            right[:, start:start + depth], left_ref[...], (((1,), (1,)), ((), ())),
             preferred_element_type=jnp.float32,
         )
         total = part if total is None else total + part
@@ -213,13 +213,15 @@
     return total.T
 
 
-def left_parts(own_ref, shared_ref):
-    return [own_ref.at[0]] + [shared_ref.at[step, 0] for step in range(shared_ref.shape[0])]
-
-
-def first_kernel(stored, group_size, width, count_ref, code_ref, panels_ref, own_ref, shared_ref, right_ref, square_ref):
+def left_parts(own_ref, shared_ref, row):
+    return [own_ref.at[row]] + [shared_ref.at[step, row] for step in range(shared_ref.shape[0])]
+
+
+def first_kernel(stored, group_size, width, count_ref, code_ref, panels_ref, own_ref, shared_ref, right_hbm, square_ref, rights, leave_sem):
     row = pl.program_id(0)
-    right_ref[...] = jnp.zeros_like(right_ref)
+    rows, depth, _ = rights.shape
+    right_ref = rights.at[row]
+    right_ref[...] = jnp.zeros(right_ref.shape, right_ref.dtype)
     half = lax.broadcasted_iota(jnp.int32, (width, 2 * width), 1) >= width
 
     def one(entry, carry):
@@ -244,16 +246,38 @@
         for inner, place, value in pieces:
             lanes = pl.ds(pl.multiple_of(lax.div(inner, 2) * 2 * width, 2 * width), 2 * width)
             lines = pl.ds(pl.multiple_of(place * width, width), width)
-            right_ref[0, lines, lanes] += value
+            right_ref[lines, lanes] += value
         return carry
 
     lax.fori_loop(0, lax.div(count_ref[row] + UNROLL - 1, UNROLL), one, 0)
-    square_ref[0] = multiply(right_ref, left_parts(own_ref, shared_ref)).astype(square_ref.dtype)
-
-
-def second_kernel(own_ref, shared_ref, right_ref, out_ref):
-    total = multiply(right_ref, left_parts(own_ref, shared_ref))
-    out_ref[0] = 3.0 * own_ref[0].astype(jnp.float32) - 2.0 * total
+    wide = 2 * width
+
+    def leave(which, part):
+        lines = pl.ds(part * wide, wide)
+        return pltpu.make_async_copy(
+            rights.at[which, lines], right_hbm.at[which, lines], leave_sem.at[which, part]
+        )
+
+    for part in range(depth // wide):
+        leave(row, part).start()
+    total = multiply(right_ref[...], left_parts(own_ref, shared_ref, 0))
+    square_ref[0] = total.astype(square_ref.dtype)
+
+    @pl.when(row == rows - 1)
+    def _():
+        for which in range(rows):
+            for part in range(depth // wide):
+                leave(which, part).wait()
+
+
+def second_kernel(own_ref, shared_ref, *refs):
+    *right_refs, out_ref = refs
+    wide = right_refs[0].shape[1]
+    for row in range(own_ref.shape[0]):
+        for part, right_ref in enumerate(right_refs):
+            lanes = slice(part * wide, (part + 1) * wide)
+            total = multiply(right_ref[row], left_parts(own_ref, shared_ref, row))
+            out_ref[row, :, lanes] = 3.0 * own_ref[row, :, lanes].astype(jnp.float32) - 2.0 * total
 
 
 def shards(density, columns):
@@ -268,14 +292,18 @@
     panels, shared = fetch(density, groups, size, span, planes)
     row_spec = pl.BlockSpec((1, width, depth), lambda i, *_: (i, 0, 0))
     shared_spec = pl.BlockSpec((groups - 1, 1, width, depth), lambda i, *_: (0, i, 0, 0))
-    right_spec = pl.BlockSpec((1, depth, stored * width), lambda i, *_: (i, 0, 0))
+    parts = depth // (2 * width)
     right, square = pl.pallas_call(
         functools.partial(first_kernel, stored, group_size, width),
         grid_spec=pltpu.PrefetchScalarGridSpec(
             num_scalar_prefetch=2,
             grid=(rows,),
             in_specs=[pl.BlockSpec(panels.shape, lambda i, *_: (0, 0, 0)), row_spec, shared_spec],
-            out_specs=[right_spec, row_spec],
+            out_specs=[pl.BlockSpec(memory_space=pl.ANY), row_spec],
+            scratch_shapes=[
+                pltpu.VMEM((rows, depth, stored * width), density.dtype),
+                pltpu.SemaphoreType.DMA((rows, parts)),
+            ],
         ),
         out_shape=[
             jax.ShapeDtypeStruct((rows, depth, stored * width), density.dtype),
@@ -283,14 +311,20 @@
         ],
         compiler_params=pltpu.CompilerParams(vmem_limit_bytes=40 * 1024 * 1024),
     )(count, codes, panels, density, shared)
+    two_spec = pl.BlockSpec((2, width, depth), lambda i: (i, 0, 0))
+    shared_two = pl.BlockSpec((groups - 1, 2, width, depth), lambda i: (0, i, 0, 0))
+    part_specs = [
+        pl.BlockSpec((2, 2 * width, stored * width), functools.partial(lambda part, i: (i, part, 0), part))
+        for part in range(parts)
+    ]
     return pl.pallas_call(
         second_kernel,
-        grid=(rows,),
-        in_specs=[row_spec, shared_spec, right_spec],
-        out_specs=row_spec,
+        grid=(rows // 2,),
+        in_specs=[two_spec, shared_two] + part_specs,
+        out_specs=two_spec,
         out_shape=jax.ShapeDtypeStruct(density.shape, jnp.float32),
         compiler_params=pltpu.CompilerParams(vmem_limit_bytes=40 * 1024 * 1024),
-    )(square, exchange(square, groups, 1), right)
+    )(square, exchange(square, groups, 1), *([right] * parts))
 
 
 def solution(mesh):

time: 142 us -> 139 us (0.979)
  Pallas kernels: 129 us -> 125 us
    pallas_call x1, Pallas kernels: 15.8 us -> 11.3 us  [shards(): pl.pallas_call(second_kernel, grid=(rows // 2,), in_specs=[two_spec, shar...]
where the time goes in v4:
time: 139 us; the launch traced here: 138 us
  Pallas kernels  125 us (90%)
  local copies, waits for them, and re-layouts  9.48 us (7%)
  other arithmetic  3.01 us (2%)
    pallas_call x1, Pallas kernels, fetch(): pl.pallas_call(body, in_specs=[pl.BlockSpec(memory_space=pltpu.VMEM)], ou...  85.3 us
    pallas_call x1, Pallas kernels, shards(): pl.pallas_call(functools.partial(first_kernel, stored, group_size, width)...  25.2 us
    pallas_call x1, Pallas kernels, shards(): pl.pallas_call(second_kernel, grid=(rows // 2,), in_specs=[two_spec, shar...  11.3 us
    unnamed x11, local copies, waits for them, and re-layouts  5.99 us
    pallas_call x1, Pallas kernels, exchange(): pl.pallas_call(functools.partial(exchange_kernel, groups), in_specs=[pl.B...  3.14 us

profile of v4, /device:TPU:0, one launch (start us, length us, event | category | flops | bytes accessed | tf_op | source)
XLA Modules:
  0.0 137.6 jit_solution(1847276082846979623)
XLA Ops:
  0.0 0.8 dynamic_slice.11
  0.8 0.1 copy.28
  0.9 0.1 add.126
  1.0 0.1 add.127
  1.1 0.8 fusion.2
  1.8 0.7 constant_dynamic-slice_fusion
  2.5 0.1 add.122
  2.6 0.8 compare_and_fusion
  3.4 0.1 copy.24
  3.5 0.1 copy.26
  3.6 0.1 reshape.88
  3.7 0.1 copy.32
  3.7 0.1 copy.35
  3.9 0.7 gather_fusion
  4.6 0.1 broadcast_select_fusion
  4.7 0.1 copy.27
  4.8 0.3 compare_reduce_fusion
  5.1 0.2 fusion
  5.3 0.1 copy.29
  5.4 0.1 copy.33
  5.5 0.1 copy.34
  5.6 0.1 copy.31
  5.7 0.1 copy.30
  5.8 0.3 reduce_window_sum.11
  6.1 0.5 select_reduce_fusion
  6.5 0.2 slice_reduce_fusion.count_ref
  6.7 0.0 copy-start.3
  6.7 1.2 copy-done.3
  8.0 85.3 %shard_map.28 = (bf16[7,8,512,128]{3,2,1,0:T(8,128)(2,1)S(1)}, bf16[1,16,64,512]{3,2,1,0:T(8,128)(2,1)S(1)}) custom-call(bf16[16,64,512]{2,1,0:T(8,128)(2,1)S(1)} %copy-done.3), custom_call_target="tpu_custom_call" | custom-call | tf_op jit(solution)/shard_map/pallas_call | solution.py:156
  93.2 0.0 copy-start.4
  93.3 1.2 copy-done.4
  94.5 25.2 %shard_map.29 = (bf16[16,512,1024]{2,1,0:T(8,128)(2,1)}, bf16[16,64,512]{2,1,0:T(8,128)(2,1)S(1)}) custom-call(s32[16]{0:T(128)S(1)} %slice_reduce_fusion.count_ref, s32[16,128]{1,0:T(8,128)S(1)} %broadcast_add_fusion.code_ref, bf16[56,512,128]{2,1,0:T(8,128)(2,1)S(1)} %bitcast.7, bf16[16,64,512]{2,1,0:T(8,128)(2,1)S(1)} %copy-done.4, ...), custom_call_target="tpu_custom_call" | custom-call | tf_op jit(solution)/shard_map/pallas_call | solution.py:296
  119.7 0.0 copy-start
  119.7 1.0 copy-done
  120.7 3.1 %shard_map.30.shared_ref = bf16[1,16,64,512]{3,2,1,0:T(8,128)(2,1)} custom-call(bf16[16,64,512]{2,1,0:T(8,128)(2,1)} %copy-done), custom_call_target="tpu_custom_call" | custom-call | tf_op jit(solution)/shard_map/pallas_call | solution.py:49
  123.8 0.0 copy-start.1
  123.9 1.2 copy-done.1
  125.1 0.0 copy-start.2
  125.1 1.2 copy-done.2
  126.3 11.3 %shard_map.31 = f32[16,64,512]{2,1,0:T(8,128)} custom-call(bf16[16,64,512]{2,1,0:T(8,128)(2,1)S(1)} %copy-done.1, bf16[1,16,64,512]{3,2,1,0:T(8,128)(2,1)S(1)} %copy-done.2, bf16[16,512,1024]{2,1,0:T(8,128)(2,1)} %get-tuple-element.12.refs_0_.refs_1_.refs_2_.refs_3_, bf16[16,512,1024]{2,1,0:T(8,128)(2,1)} %get-tuple-element.12.refs_0_.refs_1_.refs_2_.refs_3_, ...), custom_call_target="tpu_custom_call" | custom-call | tf_op jit(solution)/shard_map/pallas_call | solution.py:320
  (8 shorter events, 0.1 us)
Async XLA Ops:
  6.7 1.2 copy-start.3
  93.2 1.2 copy-start.4
  119.7 1.0 copy-start
  123.8 1.2 copy-start.1
  125.1 1.2 copy-start.2

commit v5 on v4

--- a/solution.py
+++ b/solution.py
@@ -2,6 +2,7 @@
 
 import jax
 import jax.numpy as jnp
+import numpy as np
 from jax import lax
 from jax.experimental import pallas as pl
 from jax.experimental.pallas import tpu as pltpu
@@ -81,7 +82,7 @@
     own.wait()
 
 
-def relay_kernel(groups, size, chunks, block, panels, shared, turned, own_sem, col_send, col_recv, send_sem, recv_sem):
+def relay_kernel(groups, size, chunks, block, panels, shared, turned, own_sem, col_send, col_recv, send_sem, recv_sem, held, up_send, up_recv):
     me = lax.axis_index("row")
     x_step = 1 - 2 * lax.rem(me, 2)
     y_step = 2 - 4 * lax.rem(lax.div(me, 2), 2)
@@ -103,16 +104,51 @@
         others.append(copy)
         return copy
 
+    def from_held(kind, chunk, way, slot, device):
+        lines = pl.ds(chunk * depth, depth)
+        copy = pltpu.make_async_remote_copy(
+            src_ref=held.at[way, chunk // 2], dst_ref=panels.at[slot, lines],
+            send_sem=send_sem.at[kind, chunk], recv_sem=recv_sem.at[kind, chunk],
+            device_id={"row": device}, device_id_type=pl.DeviceIdType.MESH,
+        )
+        copy.start()
+        others.append(copy)
+        return copy
+
     def pass_on(kind, chunk):
         step = steps[kind]
         sign = jnp.where(step > 0, 1, -1)
         target = lax.rem(me + 4 * sign + size, size)
         late.append(send(3 + kind, chunk, panels.at[3 + step], 3 + step - 4 * sign, target))
 
+    place = lax.rem(me, 4)
+    x_sign, y_sign = x_step, lax.div(y_step, 2)
+    x_held = lax.div(1 + x_sign, 2)
+    y_held = lax.div(1 + y_sign, 2)
+
+    def level(way, chunk):
+        lines = pl.ds(chunk * depth, depth)
+        return pltpu.make_async_remote_copy(
+            src_ref=turned.at[lines], dst_ref=held.at[way, chunk // 2],
+            send_sem=up_send.at[way, chunk // 2], recv_sem=up_recv.at[way, chunk // 2],
+            device_id={"row": above if way == 0 else below}, device_id_type=pl.DeviceIdType.MESH,
+        )
+
+    def on_level(chunk, act):
+        @pl.when(place > 0)
+        def _():
+            act(level(0, chunk))
+
+        @pl.when(place < 3)
+        def _():
+            act(level(1, chunk))
+
     late, arriving = [], []
     for chunk in range(chunks):
         for pair in range(chunk * depth, (chunk + 1) * depth):
             turn(block, turned, pair)
+        if chunk % 2 == 0:
+            on_level(chunk, lambda copy: copy.start())
         arriving.append((
             send(0, chunk, turned, 3 - x_step, x_near),
             send(1, chunk, turned, 3 - y_step, y_near),
@@ -120,23 +156,38 @@
     own = pltpu.make_async_copy(turned, panels.at[3], own_sem)
     own.start()
     col_copies = share_with_peers(groups, block, shared, col_send, col_recv)
-    corner = []
+    corner, spread = {}, {}
     lag = 2
     for chunk in range(chunks + lag):
         if chunk < chunks:
+            by_y = chunk % 4 != 1
             arriving[chunk][0].wait_recv()
-            if chunk % 2 == 0:
-                corner.append(send(2, chunk, panels.at[3 + x_step], 3 + x_step - y_step, y_near))
-            pass_on(0, chunk)
+            if by_y:
+                corner[chunk] = send(2, chunk, panels.at[3 + x_step], 3 + x_step - y_step, y_near)
+            if chunk % 2 == 1:
+                pass_on(0, chunk)
             arriving[chunk][1].wait_recv()
+            if not by_y:
+                corner[chunk] = send(2, chunk, panels.at[3 + y_step], 3 + y_step - x_step, x_near)
             if chunk % 2 == 1:
-                corner.append(send(2, chunk, panels.at[3 + y_step], 3 + y_step - x_step, x_near))
-            pass_on(1, chunk)
-        if chunk >= lag:
-            corner[chunk - lag].wait_recv()
-            pass_on(2, chunk - lag)
+                pass_on(1, chunk)
+            else:
+                on_level(chunk, lambda copy: copy.wait_recv())
+                late.append(from_held(3, chunk, x_held, 3 - x_step + 4 * x_sign, x_near))
+                spread[chunk] = from_held(4, chunk, y_held, 3 - y_step + 4 * y_sign, y_near)
+        done = chunk - lag
+        if done >= 0:
+            corner[done].wait_recv()
+            if done % 2 == 1:
+                pass_on(2, done)
+            else:
+                spread[done].wait_recv()
+                slot = 3 + y_step - 4 * y_sign
+                late.append(send(5, done, panels.at[slot], slot - x_step, x_near))
     for copy in late:
         copy.wait_recv()
+    for chunk in range(0, chunks, 2):
+        on_level(chunk, lambda copy: copy.wait_send())
     for copy in others:
         copy.wait_send()
     for copy in col_copies:
@@ -153,6 +204,13 @@
     anywhere = pl.BlockSpec(memory_space=pl.ANY)
     rows, width, depth = density.shape
     turned = (rows // 2, depth, 2 * width)
+    extra = []
+    if planes:
+        extra = [
+            pltpu.VMEM((2, chunks // 2, rows // 2 // chunks, depth, 2 * width), density.dtype),
+            pltpu.SemaphoreType.DMA((2, chunks // 2)),
+            pltpu.SemaphoreType.DMA((2, chunks // 2)),
+        ]
     panels, shared = pl.pallas_call(
         body,
         in_specs=[pl.BlockSpec(memory_space=pltpu.VMEM)],
@@ -168,7 +226,7 @@
             pltpu.SemaphoreType.DMA((groups - 1, PIECES)),
             pltpu.SemaphoreType.DMA(shape),
             pltpu.SemaphoreType.DMA(shape),
-        ],
+        ] + extra,
         compiler_params=pltpu.CompilerParams(
             collective_id=0, has_side_effects=True, vmem_limit_bytes=32 * 1024 * 1024
         ),
@@ -190,7 +248,11 @@
     live = jnp.any(equal, axis=-1)
     place = jnp.sum(jnp.where(equal, slots, 0), axis=-1)
     inner = jnp.mod(jnp.arange(stored, dtype=jnp.int32) - first, stored)[None, :, None]
-    code = ((distance[:, :, None] * group_size + slots) * stored + inner) * group_size + place
+    odd = jnp.mod(inner, 2)
+    flip = (jnp.mod(distance[:, :, None], 2) != odd).astype(jnp.int32)
+    code = (distance[:, :, None] // 2) * 256 + slots
+    code = (code * 256 + inner // 2) * 16 + place
+    code = code * 4 + flip * 2 + odd
     flat = live.reshape(rows, stored * group_size)
     code = code.reshape(rows, stored * group_size)
     order = jnp.cumsum(flat.astype(jnp.int32), axis=1)
@@ -198,6 +260,15 @@
     chosen = flat[:, None, :] & (order[:, None, :] == ranks[None, :, None])
     packed = jnp.sum(jnp.where(chosen, code[:, None, :] + 1, 0), axis=-1)
     return order[:, -1], packed - 1
+
+
+def half_factors(width, dtype):
+    high = np.arange(2 * width) >= width
+    factors = np.zeros((5, 2, width, 2 * width), np.float32)
+    for flip in range(2):
+        for odd in range(2):
+            factors[2 * flip + odd, flip] = high == bool(odd)
+    return jnp.asarray(factors, dtype)
 
 
 def multiply(right, left_refs):
@@ -217,34 +288,26 @@
     return [own_ref.at[row]] + [shared_ref.at[step, row] for step in range(shared_ref.shape[0])]
 
 
-def first_kernel(stored, group_size, width, count_ref, code_ref, panels_ref, own_ref, shared_ref, right_hbm, square_ref, rights, leave_sem):
+def first_kernel(stored, group_size, width, count_ref, code_ref, panels_ref, halves_ref, own_ref, shared_ref, right_hbm, square_ref, rights, leave_sem):
     row = pl.program_id(0)
     rows, depth, _ = rights.shape
     right_ref = rights.at[row]
     right_ref[...] = jnp.zeros(right_ref.shape, right_ref.dtype)
-    half = lax.broadcasted_iota(jnp.int32, (width, 2 * width), 1) >= width
 
     def one(entry, carry):
         pieces = []
         for part in range(UNROLL):
             raw = code_ref[row, entry * UNROLL + part]
-            real = raw >= 0
+            kind = jnp.where(raw >= 0, raw & 3, 4)
             code = jnp.maximum(raw, 0)
-            place = lax.rem(code, group_size)
-            code = lax.div(code, group_size)
-            inner = lax.rem(code, stored)
-            code = lax.div(code, stored)
-            slot = lax.rem(code, group_size)
-            source = lax.div(code, group_size)
-            value = panels_ref[lax.div(source, 2), pl.ds(pl.multiple_of(slot * width, width), width), :]
+            place, inner = (code >> 2) & 15, (code >> 6) & 255
+            slot, source = (code >> 14) & 255, code >> 22
+            value = panels_ref[source, pl.ds(pl.multiple_of(slot * width, width), width), :]
             swapped = jnp.concatenate([value[:, width:], value[:, :width]], axis=1)
-            odd = lax.rem(inner, 2)
-            same = jnp.full(value.shape, lax.rem(source, 2), jnp.int32) == odd
-            value = jnp.where(same, value, swapped)
-            mine = (half == (jnp.full(value.shape, odd, jnp.int32) == 1)) & jnp.full(value.shape, real)
-            pieces.append((inner, place, jnp.where(mine, value, jnp.zeros_like(value))))
+            keep, turn_over = halves_ref[kind, 0], halves_ref[kind, 1]
+            pieces.append((inner, place, value * keep + swapped * turn_over))
         for inner, place, value in pieces:
-            lanes = pl.ds(pl.multiple_of(lax.div(inner, 2) * 2 * width, 2 * width), 2 * width)
+            lanes = pl.ds(pl.multiple_of(inner * 2 * width, 2 * width), 2 * width)
             lines = pl.ds(pl.multiple_of(place * width, width), width)
             right_ref[lines, lanes] += value
         return carry
@@ -290,6 +353,7 @@
     size = lax.axis_size("row")
     planes = (size, groups, span) == (16, 2, 3)
     panels, shared = fetch(density, groups, size, span, planes)
+    halves = half_factors(width, density.dtype)
     row_spec = pl.BlockSpec((1, width, depth), lambda i, *_: (i, 0, 0))
     shared_spec = pl.BlockSpec((groups - 1, 1, width, depth), lambda i, *_: (0, i, 0, 0))
     parts = depth // (2 * width)
@@ -298,7 +362,11 @@
         grid_spec=pltpu.PrefetchScalarGridSpec(
             num_scalar_prefetch=2,
             grid=(rows,),
-            in_specs=[pl.BlockSpec(panels.shape, lambda i, *_: (0, 0, 0)), row_spec, shared_spec],
+            in_specs=[
+                pl.BlockSpec(panels.shape, lambda i, *_: (0, 0, 0)),
+                pl.BlockSpec(halves.shape, lambda i, *_: (0, 0, 0, 0)),
+                row_spec, shared_spec,
+            ],
             out_specs=[pl.BlockSpec(memory_space=pl.ANY), row_spec],
             scratch_shapes=[
                 pltpu.VMEM((rows, depth, stored * width), density.dtype),
@@ -310,7 +378,7 @@
             jax.ShapeDtypeStruct(density.shape, density.dtype),
         ],
         compiler_params=pltpu.CompilerParams(vmem_limit_bytes=40 * 1024 * 1024),
-    )(count, codes, panels, density, shared)
+    )(count, codes, panels, halves, density, shared)
     two_spec = pl.BlockSpec((2, width, depth), lambda i: (i, 0, 0))
     shared_two = pl.BlockSpec((groups - 1, 2, width, depth), lambda i: (0, i, 0, 0))
     part_specs = [

time: 139 us -> 120 us (0.86)
  Pallas kernels: 125 us -> 105 us
    pallas_call x1, Pallas kernels: 85.3 us -> 65.8 us  [fetch(): pl.pallas_call(body, in_specs=[pl.BlockSpec(memory_space=pltpu.VMEM)], ou...]
    unnamed x11 -> x13, local copies, waits for them, and re-layouts: 5.99 us -> 6.91 us
where the time goes in v5:
time: 120 us; the launch traced here: 119 us
  Pallas kernels  105 us (88%)
  local copies, waits for them, and re-layouts  10.6 us (9%)
  other arithmetic  3.03 us (3%)
    pallas_call x1, Pallas kernels, fetch(): pl.pallas_call(body, in_specs=[pl.BlockSpec(memory_space=pltpu.VMEM)], ou...  65.8 us
    pallas_call x1, Pallas kernels, shards(): pl.pallas_call(functools.partial(first_kernel, stored, group_size, width)...  25.1 us
    pallas_call x1, Pallas kernels, shards(): pl.pallas_call(second_kernel, grid=(rows // 2,), in_specs=[two_spec, shar...  11.3 us
    unnamed x13, local copies, waits for them, and re-layouts  6.91 us
    pallas_call x1, Pallas kernels, exchange(): pl.pallas_call(functools.partial(exchange_kernel, groups), in_specs=[pl.B...  3.14 us

profile of v5, /device:TPU:0, one launch (start us, length us, event | category | flops | bytes accessed | tf_op | source)
XLA Modules:
  0.0 119.1 jit_solution(14615130612095488846)
XLA Ops:
  0.0 0.8 dynamic_slice.11
  0.8 0.1 copy.30
  0.9 0.1 add.188
  1.0 0.1 add.189
  1.1 0.7 constant_dynamic-slice_fusion
  1.8 0.1 add.198
  1.8 0.1 add.199
  1.9 0.1 add.184
  2.0 0.8 compare_and_fusion
  2.8 0.1 copy.26
  2.9 0.1 copy.28
  3.0 0.1 reshape.179
  3.1 0.8 fusion.2
  3.9 0.1 copy.34
  3.9 0.1 copy.37
  4.0 0.1 copy.38
  4.2 0.7 gather_fusion
  4.9 0.1 broadcast_select_fusion
  5.0 0.1 copy.29
  5.1 0.3 compare_reduce_fusion
  5.3 0.2 fusion
  5.6 0.1 copy.31
  5.7 0.1 copy.35
  5.8 0.1 copy.36
  5.9 0.1 copy.33
  6.0 0.1 copy.32
  6.0 0.3 reduce_window_sum.11
  6.3 0.5 select_reduce_fusion
  6.8 0.2 slice_reduce_fusion.count_ref
  7.0 0.0 copy-start.3
  7.0 1.2 %copy-done.3 = bf16[16,64,512]{2,1,0:T(8,128)(2,1)S(1)} copy-done((bf16[16,64,512]{2,1,0:T(8,128)(2,1)S(1)}, bf16[16,64,512]{2,1,0:T(8,128)(2,1)}, u32[]{:S(2)}) %copy-start.3) | copy-done | bytes 1048600
  8.2 65.8 %shard_map.37 = (bf16[7,8,512,128]{3,2,1,0:T(8,128)(2,1)S(1)}, bf16[1,16,64,512]{3,2,1,0:T(8,128)(2,1)S(1)}) custom-call(bf16[16,64,512]{2,1,0:T(8,128)(2,1)S(1)} %copy-done.3), custom_call_target="tpu_custom_call" | custom-call | tf_op jit(solution)/shard_map/pallas_call | solution.py:214
  74.0 0.0 copy-start.4
  74.0 1.2 %copy-done.4 = bf16[16,64,512]{2,1,0:T(8,128)(2,1)S(1)} copy-done((bf16[16,64,512]{2,1,0:T(8,128)(2,1)S(1)}, bf16[16,64,512]{2,1,0:T(8,128)(2,1)}, u32[]{:S(2)}) %copy-start.4) | copy-done | bytes 1048600
  75.2 0.0 copy-start.5
  75.2 0.9 copy-done.5
  76.1 25.1 %shard_map.38 = (bf16[16,512,1024]{2,1,0:T(8,128)(2,1)}, bf16[16,64,512]{2,1,0:T(8,128)(2,1)S(1)}) custom-call(s32[16]{0:T(128)S(1)} %slice_reduce_fusion.count_ref, s32[16,128]{1,0:T(8,128)S(1)} %broadcast_add_fusion.code_ref, bf16[56,512,128]{2,1,0:T(8,128)(2,1)S(1)} %bitcast.9, bf16[5,2,64,128]{3,2,1,0:T(8,128)(2,1)S(1)} %copy-done.5, ...), custom_call_target="tpu_custom_call" | custom-call | tf_op jit(solution)/shard_map/pallas_call | solution.py:360
  101.2 0.0 copy-start
  101.2 1.0 copy-done
  102.2 3.1 %shard_map.39.shared_ref = bf16[1,16,64,512]{3,2,1,0:T(8,128)(2,1)} custom-call(bf16[16,64,512]{2,1,0:T(8,128)(2,1)} %copy-done), custom_call_target="tpu_custom_call" | custom-call | tf_op jit(solution)/shard_map/pallas_call | solution.py:50
  105.3 0.0 copy-start.1
  105.4 1.2 %copy-done.1 = bf16[16,64,512]{2,1,0:T(8,128)(2,1)S(1)} copy-done((bf16[16,64,512]{2,1,0:T(8,128)(2,1)S(1)}, bf16[16,64,512]{2,1,0:T(8,128)(2,1)}, u32[]{:S(2)}) %copy-start.1) | copy-done | bytes 1048600
  106.6 0.0 copy-start.2
  106.6 1.2 %copy-done.2 = bf16[1,16,64,512]{3,2,1,0:T(8,128)(2,1)S(1)} copy-done((bf16[1,16,64,512]{3,2,1,0:T(8,128)(2,1)S(1)}, bf16[1,16,64,512]{3,2,1,0:T(8,128)(2,1)}, u32[]{:S(2)}) %copy-start.2) | copy-done | bytes 1048600
  107.8 11.3 %shard_map.40 = f32[16,64,512]{2,1,0:T(8,128)} custom-call(bf16[16,64,512]{2,1,0:T(8,128)(2,1)S(1)} %copy-done.1, bf16[1,16,64,512]{3,2,1,0:T(8,128)(2,1)S(1)} %copy-done.2, bf16[16,512,1024]{2,1,0:T(8,128)(2,1)} %get-tuple-element.12.refs_0_.refs_1_.refs_2_.refs_3_, bf16[16,512,1024]{2,1,0:T(8,128)(2,1)} %get-tuple-element.12.refs_0_.refs_1_.refs_2_.refs_3_, ...), custom_call_target="tpu_custom_call" | custom-call | tf_op jit(solution)/shard_map/pallas_call | solution.py:388
  (9 shorter events, 0.1 us)
Async XLA Ops:
  7.0 1.2 %copy-start.3 = (bf16[16,64,512]{2,1,0:T(8,128)(2,1)S(1)}, bf16[16,64,512]{2,1,0:T(8,128)(2,1)}, u32[]{:S(2)}) copy-start(bf16[16,64,512]{2,1,0:T(8,128)(2,1)} %own_ref.1) | copy-start | bytes 3145732
  74.0 1.2 %copy-start.4 = (bf16[16,64,512]{2,1,0:T(8,128)(2,1)S(1)}, bf16[16,64,512]{2,1,0:T(8,128)(2,1)}, u32[]{:S(2)}) copy-start(bf16[16,64,512]{2,1,0:T(8,128)(2,1)} %own_ref.1) | copy-start | bytes 3145732
  75.2 0.9 copy-start.5
  101.2 1.0 copy-start
  105.3 1.2 %copy-start.1 = (bf16[16,64,512]{2,1,0:T(8,128)(2,1)S(1)}, bf16[16,64,512]{2,1,0:T(8,128)(2,1)}, u32[]{:S(2)}) copy-start(bf16[16,64,512]{2,1,0:T(8,128)(2,1)} %copy-done) | copy-start | bytes 3145732
  106.6 1.2 %copy-start.2 = (bf16[1,16,64,512]{3,2,1,0:T(8,128)(2,1)S(1)}, bf16[1,16,64,512]{3,2,1,0:T(8,128)(2,1)}, u32[]{:S(2)}) copy-start(bf16[1,16,64,512]{3,2,1,0:T(8,128)(2,1)} %shard_map.39.shared_ref) | copy-start | bytes 3145732

commit v6 on v5

--- a/solution.py
+++ b/solution.py
@@ -2,7 +2,6 @@
 
 import jax
 import jax.numpy as jnp
-import numpy as np
 from jax import lax
 from jax.experimental import pallas as pl
 from jax.experimental.pallas import tpu as pltpu
@@ -11,6 +10,7 @@
 REACH = 48
 UNROLL = 4
 PIECES = 8
+LIMIT = 8 * 1024 * 1024
 
 
 def greet(devices):
@@ -24,7 +24,7 @@
     return [{"col": lax.rem(lax.axis_index("col") + step, groups)} for step in range(1, groups)]
 
 
-def share_with_peers(groups, block, shared, send_sem, recv_sem):
+def share_with_peers(groups, block, shared, first, send_sem, recv_sem):
     copies = []
     chunks = send_sem.shape[1]
     depth = block.shape[0] // chunks
@@ -32,7 +32,7 @@
         for chunk in range(chunks):
             lines = pl.ds(chunk * depth, depth)
             copies.append(pltpu.make_async_remote_copy(
-                src_ref=block.at[lines], dst_ref=shared.at[groups - 2 - step, lines],
+                src_ref=block.at[lines], dst_ref=shared.at[first + groups - 2 - step, lines],
                 send_sem=send_sem.at[step, chunk], recv_sem=recv_sem.at[step, chunk],
                 device_id=peer, device_id_type=pl.DeviceIdType.MESH,
             ))
@@ -42,18 +42,20 @@
 
 def exchange_kernel(groups, block, shared, send_sem, recv_sem):
     greet(col_peers(groups))
-    for copy in share_with_peers(groups, block, shared, send_sem, recv_sem):
+    for copy in share_with_peers(groups, block, shared, 0, send_sem, recv_sem):
         copy.wait()
 
 
 def exchange(block, groups, collective_id):
     return pl.pallas_call(
         functools.partial(exchange_kernel, groups),
-        in_specs=[pl.BlockSpec(memory_space=pl.ANY)],
-        out_specs=pl.BlockSpec(memory_space=pl.ANY),
+        in_specs=[pl.BlockSpec(memory_space=pltpu.VMEM)],
+        out_specs=pl.BlockSpec(memory_space=pltpu.VMEM),
         out_shape=jax.ShapeDtypeStruct((groups - 1,) + block.shape, block.dtype),
         scratch_shapes=[pltpu.SemaphoreType.DMA((groups - 1, PIECES))] * 2,
-        compiler_params=pltpu.CompilerParams(collective_id=collective_id, has_side_effects=True),
+        compiler_params=pltpu.CompilerParams(
+            collective_id=collective_id, has_side_effects=True, vmem_limit_bytes=LIMIT
+        ),
     )(block)
 
 
@@ -66,7 +68,8 @@
     me = lax.axis_index("row")
     offsets = [d for d in range(-span, span + 1) if d != 0]
     greet([{"row": lax.rem(me + d + size, size)} for d in offsets] + col_peers(groups))
-    copies = share_with_peers(groups, block, shared, col_send, col_recv)
+    copies = share_with_peers(groups, block, shared, 1, col_send, col_recv)
+    shared[0] = block[...]
     for pair in range(turned.shape[0]):
         turn(block, turned, pair)
     own = pltpu.make_async_copy(turned, panels.at[span], own_sem)
@@ -155,7 +158,8 @@
         ))
     own = pltpu.make_async_copy(turned, panels.at[3], own_sem)
     own.start()
-    col_copies = share_with_peers(groups, block, shared, col_send, col_recv)
+    col_copies = share_with_peers(groups, block, shared, 1, col_send, col_recv)
+    shared[0] = block[...]
     corner, spread = {}, {}
     lag = 2
     for chunk in range(chunks + lag):
@@ -201,7 +205,7 @@
         body, shape = functools.partial(relay_kernel, groups, size, chunks), (6, chunks)
     else:
         body, shape = functools.partial(direct_kernel, groups, size, span), (2 * span,)
-    anywhere = pl.BlockSpec(memory_space=pl.ANY)
+    inside = pl.BlockSpec(memory_space=pltpu.VMEM)
     rows, width, depth = density.shape
     turned = (rows // 2, depth, 2 * width)
     extra = []
@@ -213,11 +217,11 @@
         ]
     panels, shared = pl.pallas_call(
         body,
-        in_specs=[pl.BlockSpec(memory_space=pltpu.VMEM)],
-        out_specs=[anywhere, anywhere],
+        in_specs=[inside],
+        out_specs=[inside, inside],
         out_shape=[
             jax.ShapeDtypeStruct((2 * span + 1,) + turned, density.dtype),
-            jax.ShapeDtypeStruct((groups - 1,) + density.shape, density.dtype),
+            jax.ShapeDtypeStruct((groups,) + density.shape, density.dtype),
         ],
         scratch_shapes=[
             pltpu.VMEM(turned, density.dtype),
@@ -228,7 +232,7 @@
             pltpu.SemaphoreType.DMA(shape),
         ] + extra,
         compiler_params=pltpu.CompilerParams(
-            collective_id=0, has_side_effects=True, vmem_limit_bytes=32 * 1024 * 1024
+            collective_id=0, has_side_effects=True, vmem_limit_bytes=LIMIT
         ),
     )(density)
     return panels.reshape((-1,) + turned[1:]), shared
@@ -262,21 +266,21 @@
     return order[:, -1], packed - 1
 
 
-def half_factors(width, dtype):
-    high = np.arange(2 * width) >= width
-    factors = np.zeros((5, 2, width, 2 * width), np.float32)
+def fill_halves(halves_ref, width):
+    lane = lax.broadcasted_iota(jnp.int32, (width, 2 * width), 1)
+    high = jnp.where(lane >= width, 1.0, 0.0)
+    halves_ref[...] = jnp.zeros(halves_ref.shape, halves_ref.dtype)
     for flip in range(2):
         for odd in range(2):
-            factors[2 * flip + odd, flip] = high == bool(odd)
-    return jnp.asarray(factors, dtype)
-
-
-def multiply(right, left_refs):
+            halves_ref[2 * flip + odd, flip] = (high if odd else 1.0 - high).astype(halves_ref.dtype)
+
+
+def multiply(right_ref, left_refs):
     depth = left_refs[0].shape[-1]
     total, start = None, 0
     for left_ref in left_refs:
         part = lax.dot_general(
-            right[:, start:start + depth], left_ref[...], (((1,), (1,)), ((), ())),
+            right_ref[:, start:start + depth], left_ref[...], (((1,), (1,)), ((), ())),
             preferred_element_type=jnp.float32,
         )
         total = part if total is None else total + part
@@ -284,16 +288,42 @@
     return total.T
 
 
-def left_parts(own_ref, shared_ref, row):
-    return [own_ref.at[row]] + [shared_ref.at[step, row] for step in range(shared_ref.shape[0])]
-
-
-def first_kernel(stored, group_size, width, count_ref, code_ref, panels_ref, halves_ref, own_ref, shared_ref, right_hbm, square_ref, rights, leave_sem):
-    row = pl.program_id(0)
+def first_kernel(stored, group_size, width, count_ref, code_ref, panels_ref, left_ref, rights, square_ref, halves_ref):
     rows, depth, _ = rights.shape
-    right_ref = rights.at[row]
-    right_ref[...] = jnp.zeros(right_ref.shape, right_ref.dtype)
-
+    fill_halves(halves_ref, width)
+
+    def one_row(row, carry):
+        right_ref = rights.at[row]
+        right_ref[...] = jnp.zeros(right_ref.shape, right_ref.dtype)
+        assemble(count_ref, code_ref, panels_ref, halves_ref, row, right_ref, width)
+        total = multiply(right_ref, [left_ref.at[group, row] for group in range(left_ref.shape[0])])
+        square_ref[row] = total.astype(square_ref.dtype)
+        return carry
+
+    lax.fori_loop(0, rows, one_row, 0)
+
+
+def second_kernel(own_ref, shared_ref, rights, out_hbm, out_ref, out_sem):
+    rows = own_ref.shape[0]
+
+    def leave(row):
+        return pltpu.make_async_copy(out_ref.at[row], out_hbm.at[row], out_sem.at[row])
+
+    def one_row(row, carry):
+        left = [own_ref.at[row]] + [shared_ref.at[step, row] for step in range(shared_ref.shape[0])]
+        out_ref[row] = 3.0 * own_ref[row].astype(jnp.float32) - 2.0 * multiply(rights.at[row], left)
+        leave(row).start()
+        return carry
+
+    def done(row, carry):
+        leave(row).wait()
+        return carry
+
+    lax.fori_loop(0, rows, one_row, 0)
+    lax.fori_loop(0, rows, done, 0)
+
+
+def assemble(count_ref, code_ref, panels_ref, halves_ref, row, right_ref, width):
     def one(entry, carry):
         pieces = []
         for part in range(UNROLL):
@@ -313,34 +343,6 @@
         return carry
 
     lax.fori_loop(0, lax.div(count_ref[row] + UNROLL - 1, UNROLL), one, 0)
-    wide = 2 * width
-
-    def leave(which, part):
-        lines = pl.ds(part * wide, wide)
-        return pltpu.make_async_copy(
-            rights.at[which, lines], right_hbm.at[which, lines], leave_sem.at[which, part]
-        )
-
-    for part in range(depth // wide):
-        leave(row, part).start()
-    total = multiply(right_ref[...], left_parts(own_ref, shared_ref, 0))
-    square_ref[0] = total.astype(square_ref.dtype)
-
-    @pl.when(row == rows - 1)
-    def _():
-        for which in range(rows):
-            for part in range(depth // wide):
-                leave(which, part).wait()
-
-
-def second_kernel(own_ref, shared_ref, *refs):
-    *right_refs, out_ref = refs
-    wide = right_refs[0].shape[1]
-    for row in range(own_ref.shape[0]):
-        for part, right_ref in enumerate(right_refs):
-            lanes = slice(part * wide, (part + 1) * wide)
-            total = multiply(right_ref[row], left_parts(own_ref, shared_ref, row))
-            out_ref[row, :, lanes] = 3.0 * own_ref[row, :, lanes].astype(jnp.float32) - 2.0 * total
 
 
 def shards(density, columns):
@@ -352,47 +354,31 @@
     count, codes = live_list(columns, rows, width, group_size, span)
     size = lax.axis_size("row")
     planes = (size, groups, span) == (16, 2, 3)
-    panels, shared = fetch(density, groups, size, span, planes)
-    halves = half_factors(width, density.dtype)
-    row_spec = pl.BlockSpec((1, width, depth), lambda i, *_: (i, 0, 0))
-    shared_spec = pl.BlockSpec((groups - 1, 1, width, depth), lambda i, *_: (0, i, 0, 0))
-    parts = depth // (2 * width)
+    panels, left = fetch(density, groups, size, span, planes)
+    inside = pl.BlockSpec(memory_space=pltpu.VMEM)
+    scalars = pl.BlockSpec(memory_space=pltpu.SMEM)
     right, square = pl.pallas_call(
         functools.partial(first_kernel, stored, group_size, width),
-        grid_spec=pltpu.PrefetchScalarGridSpec(
-            num_scalar_prefetch=2,
-            grid=(rows,),
-            in_specs=[
-                pl.BlockSpec(panels.shape, lambda i, *_: (0, 0, 0)),
-                pl.BlockSpec(halves.shape, lambda i, *_: (0, 0, 0, 0)),
-                row_spec, shared_spec,
-            ],
-            out_specs=[pl.BlockSpec(memory_space=pl.ANY), row_spec],
-            scratch_shapes=[
-                pltpu.VMEM((rows, depth, stored * width), density.dtype),
-                pltpu.SemaphoreType.DMA((rows, parts)),
-            ],
-        ),
+        in_specs=[scalars, scalars, inside, inside],
+        out_specs=[inside, inside],
         out_shape=[
             jax.ShapeDtypeStruct((rows, depth, stored * width), density.dtype),
             jax.ShapeDtypeStruct(density.shape, density.dtype),
         ],
-        compiler_params=pltpu.CompilerParams(vmem_limit_bytes=40 * 1024 * 1024),
-    )(count, codes, panels, halves, density, shared)
-    two_spec = pl.BlockSpec((2, width, depth), lambda i: (i, 0, 0))
-    shared_two = pl.BlockSpec((groups - 1, 2, width, depth), lambda i: (0, i, 0, 0))
-    part_specs = [
-        pl.BlockSpec((2, 2 * width, stored * width), functools.partial(lambda part, i: (i, part, 0), part))
-        for part in range(parts)
-    ]
+        scratch_shapes=[pltpu.VMEM((5, 2, width, 2 * width), density.dtype)],
+        compiler_params=pltpu.CompilerParams(vmem_limit_bytes=LIMIT),
+    )(count, codes, panels, left)
     return pl.pallas_call(
         second_kernel,
-        grid=(rows // 2,),
-        in_specs=[two_spec, shared_two] + part_specs,
-        out_specs=two_spec,
+        in_specs=[inside, inside, inside],
+        out_specs=pl.BlockSpec(memory_space=pl.ANY),
         out_shape=jax.ShapeDtypeStruct(density.shape, jnp.float32),
-        compiler_params=pltpu.CompilerParams(vmem_limit_bytes=40 * 1024 * 1024),
-    )(square, exchange(square, groups, 1), *([right] * parts))
+        scratch_shapes=[
+            pltpu.VMEM(density.shape, jnp.float32),
+            pltpu.SemaphoreType.DMA((rows,)),
+        ],
+        compiler_params=pltpu.CompilerParams(vmem_limit_bytes=LIMIT),
+    )(square, exchange(square, groups, 1), right)
 
 
 def solution(mesh):

time: 120 us -> 109 us (0.908)
  local copies, waits for them, and re-layouts: 10.6 us -> 5.09 us
  Pallas kernels: 105 us -> 101 us
    unnamed x13 -> x3, local copies, waits for them, and re-layouts: 6.91 us -> 1.37 us
    pallas_call x2, Pallas kernels: 77.1 us -> 74.1 us  [the longest x1 65.8 us: fetch(): pl.pallas_call(body, in_specs=[inside], out_specs=[inside, inside], out_s...]
    pallas_call x1, Pallas kernels: 25.1 us -> 23.8 us  [shards(): pl.pallas_call(functools.partial(first_kernel, stored, group_size, width)...]
where the time goes in v6:
time: 109 us
  Pallas kernels  101 us (93%)
  local copies, waits for them, and re-layouts  5.09 us (5%)
  other arithmetic  3.03 us (3%)
    pallas_call x1, Pallas kernels, fetch(): pl.pallas_call(body, in_specs=[inside], out_specs=[inside, inside], out_s...  65.8 us
    pallas_call x1, Pallas kernels, shards(): pl.pallas_call(functools.partial(first_kernel, stored, group_size, width)...  23.8 us
    pallas_call x1, Pallas kernels, shards(): pl.pallas_call(second_kernel, in_specs=[inside, inside, inside], out_spec...  8.35 us
    pallas_call x1, Pallas kernels, exchange(): pl.pallas_call(functools.partial(exchange_kernel, groups), in_specs=[pl.B...  2.82 us

profile of v6, /device:TPU:0, one launch (start us, length us, event | category | flops | bytes accessed | tf_op | source)
XLA Modules:
  0.0 109.0 jit_solution(15156083045697270533)
XLA Ops:
  0.0 0.8 dynamic_slice.11
  0.8 0.1 copy.29
  0.9 0.1 add.188
  1.0 0.1 add.189
  1.1 0.7 constant_dynamic-slice_fusion
  1.8 0.1 add.198
  1.8 0.1 add.199
  1.9 0.1 add.184
  2.0 0.8 compare_and_fusion
  2.8 0.1 copy.25
  2.9 0.1 copy.27
  3.0 0.1 reshape.179
  3.1 0.8 fusion.2
  3.9 0.1 copy.33
  3.9 0.1 copy.36
  4.0 0.1 copy.37
  4.2 0.7 gather_fusion
  4.9 0.1 broadcast_select_fusion
  5.0 0.1 copy.28
  5.1 0.3 compare_reduce_fusion
  5.3 0.2 fusion
  5.6 0.1 copy.30
  5.7 0.1 copy.34
  5.8 0.1 copy.35
  5.9 0.1 copy.32
  6.0 0.1 copy.31
  6.0 0.3 reduce_window_sum.11
  6.3 0.5 select_reduce_fusion
  6.8 0.2 slice_reduce_fusion.count_ref
  7.0 0.0 copy-start
  7.0 1.2 %copy-done = bf16[16,64,512]{2,1,0:T(8,128)(2,1)S(1)} copy-done((bf16[16,64,512]{2,1,0:T(8,128)(2,1)S(1)}, bf16[16,64,512]{2,1,0:T(8,128)(2,1)}, u32[]{:S(2)}) %copy-start) | copy-done | bytes 1048600
  8.2 65.8 %shard_map.28 = (bf16[7,8,512,128]{3,2,1,0:T(8,128)(2,1)S(1)}, bf16[2,16,64,512]{3,2,1,0:T(8,128)(2,1)S(1)}) custom-call(bf16[16,64,512]{2,1,0:T(8,128)(2,1)S(1)} %copy-done), custom_call_target="tpu_custom_call" | custom-call | tf_op jit(solution)/shard_map/pallas_call | solution.py:218
  74.0 23.8 %shard_map.29 = (bf16[16,512,1024]{2,1,0:T(8,128)(2,1)S(1)}, bf16[16,64,512]{2,1,0:T(8,128)(2,1)S(1)}) custom-call(s32[16]{0:T(128)S(1)} %slice_reduce_fusion.count_ref, s32[16,128]{1,0:T(8,128)S(1)} %broadcast_add_fusion.code_ref, bf16[56,512,128]{2,1,0:T(8,128)(2,1)S(1)} %bitcast.9, bf16[2,16,64,512]{3,2,1,0:T(8,128)(2,1)S(1)} %get-tuple-element.10.left_ref), custom_call_target="tpu_custom_call" | custom-call | tf_op jit(solution)/shard_map/pallas_call | solution.py:360
  97.9 2.8 %shard_map.30.shared_ref = bf16[1,16,64,512]{3,2,1,0:T(8,128)(2,1)S(1)} custom-call(bf16[16,64,512]{2,1,0:T(8,128)(2,1)S(1)} %get-tuple-element.11.block.own_ref), custom_call_target="tpu_custom_call" | custom-call | tf_op jit(solution)/shard_map/pallas_call | solution.py:50
  100.7 8.3 %shard_map.31 = f32[16,64,512]{2,1,0:T(8,128)} custom-call(bf16[16,64,512]{2,1,0:T(8,128)(2,1)S(1)} %get-tuple-element.11.block.own_ref, bf16[1,16,64,512]{3,2,1,0:T(8,128)(2,1)S(1)} %shard_map.30.shared_ref, bf16[16,512,1024]{2,1,0:T(8,128)(2,1)S(1)} %get-tuple-element.12.rights), custom_call_target="tpu_custom_call" | custom-call | tf_op jit(solution)/shard_map/pallas_call | solution.py:371
  (9 shorter events, 0.1 us)
Async XLA Ops:
  7.0 1.2 %copy-start = (bf16[16,64,512]{2,1,0:T(8,128)(2,1)S(1)}, bf16[16,64,512]{2,1,0:T(8,128)(2,1)}, u32[]{:S(2)}) copy-start(bf16[16,64,512]{2,1,0:T(8,128)(2,1)} %block.1) | copy-start | bytes 3145732

commit v7 on v6

--- a/solution.py
+++ b/solution.py
@@ -8,7 +8,7 @@
 from jax.sharding import PartitionSpec as P
 
 REACH = 48
-UNROLL = 4
+UNROLL = 8
 PIECES = 8
 LIMIT = 8 * 1024 * 1024
 
@@ -257,13 +257,18 @@
     code = (distance[:, :, None] // 2) * 256 + slots
     code = (code * 256 + inner // 2) * 16 + place
     code = code * 4 + flip * 2 + odd
-    flat = live.reshape(rows, stored * group_size)
-    code = code.reshape(rows, stored * group_size)
-    order = jnp.cumsum(flat.astype(jnp.int32), axis=1)
-    ranks = jnp.arange(1, stored * group_size + 1, dtype=jnp.int32)
-    chosen = flat[:, None, :] & (order[:, None, :] == ranks[None, :, None])
-    packed = jnp.sum(jnp.where(chosen, code[:, None, :] + 1, 0), axis=-1)
-    return order[:, -1], packed - 1
+    length = stored * group_size // 2
+
+    def by_parity(values):
+        return values.reshape(rows, stored // 2, 2, group_size).transpose(0, 2, 1, 3).reshape(rows, 2, length)
+
+    flat, code = by_parity(live), by_parity(code)
+    order = jnp.cumsum(flat.astype(jnp.int32), axis=2)
+    ranks = jnp.arange(1, length + 1, dtype=jnp.int32)
+    wanted_rank = jnp.minimum(ranks, order[:, :, -1:])
+    chosen = flat[:, :, None, :] & (order[:, :, None, :] == wanted_rank[:, :, :, None])
+    packed = jnp.sum(jnp.where(chosen, code[:, :, None, :], 0), axis=-1)
+    return order[:, :, -1].reshape(-1), packed.reshape(2 * rows, length)
 
 
 def fill_halves(halves_ref, width):
@@ -324,25 +329,29 @@
 
 
 def assemble(count_ref, code_ref, panels_ref, halves_ref, row, right_ref, width):
-    def one(entry, carry):
-        pieces = []
-        for part in range(UNROLL):
-            raw = code_ref[row, entry * UNROLL + part]
-            kind = jnp.where(raw >= 0, raw & 3, 4)
-            code = jnp.maximum(raw, 0)
-            place, inner = (code >> 2) & 15, (code >> 6) & 255
-            slot, source = (code >> 14) & 255, code >> 22
-            value = panels_ref[source, pl.ds(pl.multiple_of(slot * width, width), width), :]
-            swapped = jnp.concatenate([value[:, width:], value[:, :width]], axis=1)
-            keep, turn_over = halves_ref[kind, 0], halves_ref[kind, 1]
-            pieces.append((inner, place, value * keep + swapped * turn_over))
-        for inner, place, value in pieces:
-            lanes = pl.ds(pl.multiple_of(inner * 2 * width, 2 * width), 2 * width)
-            lines = pl.ds(pl.multiple_of(place * width, width), width)
-            right_ref[lines, lanes] += value
-        return carry
-
-    lax.fori_loop(0, lax.div(count_ref[row] + UNROLL - 1, UNROLL), one, 0)
+    for parity in range(2):
+        line = 2 * row + parity
+
+        def one(entry, carry):
+            pieces = []
+            for part in range(UNROLL):
+                code = code_ref[line, entry * UNROLL + part]
+                kind = code & 3
+                place, inner = (code >> 2) & 15, (code >> 6) & 255
+                slot, source = (code >> 14) & 255, code >> 22
+                value = panels_ref[source, pl.ds(pl.multiple_of(slot * width, width), width), :]
+                swapped = jnp.concatenate([value[:, width:], value[:, :width]], axis=1)
+                value = value * halves_ref[kind, 0] + swapped * halves_ref[kind, 1]
+                lanes = pl.ds(pl.multiple_of(inner * 2 * width, 2 * width), 2 * width)
+                lines = pl.ds(pl.multiple_of(place * width, width), width)
+                if parity == 1:
+                    value = value + right_ref[lines, lanes]
+                pieces.append((lines, lanes, value))
+            for lines, lanes, value in pieces:
+                right_ref[lines, lanes] = value
+            return carry
+
+        lax.fori_loop(0, lax.div(count_ref[line] + UNROLL - 1, UNROLL), one, 0)
 
 
 def shards(density, columns):
@@ -365,7 +374,7 @@
             jax.ShapeDtypeStruct((rows, depth, stored * width), density.dtype),
             jax.ShapeDtypeStruct(density.shape, density.dtype),
         ],
-        scratch_shapes=[pltpu.VMEM((5, 2, width, 2 * width), density.dtype)],
+        scratch_shapes=[pltpu.VMEM((4, 2, width, 2 * width), density.dtype)],
         compiler_params=pltpu.CompilerParams(vmem_limit_bytes=LIMIT),
     )(count, codes, panels, left)
     return pl.pallas_call(

time: 109 us -> 106 us (0.972)
  Pallas kernels: 101 us -> 97.1 us
    pallas_call x1, Pallas kernels: 23.8 us -> 20.2 us  [shards(): pl.pallas_call(functools.partial(first_kernel, stored, group_size, width)...]
where the time goes in v7:
time: 106 us
  Pallas kernels  97.1 us (92%)
  local copies, waits for them, and re-layouts  4.8 us (5%)
  other arithmetic  3.89 us (4%)
    pallas_call x1, Pallas kernels, fetch(): pl.pallas_call(body, in_specs=[inside], out_specs=[inside, inside], out_s...  65.8 us
    pallas_call x1, Pallas kernels, shards(): pl.pallas_call(functools.partial(first_kernel, stored, group_size, width)...  20.2 us
    pallas_call x1, Pallas kernels, shards(): pl.pallas_call(second_kernel, in_specs=[inside, inside, inside], out_spec...  8.35 us
    pallas_call x1, Pallas kernels, exchange(): pl.pallas_call(functools.partial(exchange_kernel, groups), in_specs=[pl.B...  2.82 us

profile of v7, /device:TPU:0, one launch (start us, length us, event | category | flops | bytes accessed | tf_op | source)
XLA Modules:
  0.0 106.0 jit_solution(9702468695432828589)
XLA Ops:
  0.0 0.8 dynamic_slice.11
  0.8 0.1 copy.28
  0.9 0.7 constant_dynamic-slice_fusion
  1.6 0.8 compare_and_fusion
  2.4 0.1 copy.24
  2.5 0.1 copy.26
  2.6 0.1 reshape.131
  2.7 0.8 fusion.2
  3.5 0.1 copy.40
  3.6 0.7 gather_fusion
  4.3 0.1 broadcast_select_fusion
  4.4 0.1 copy.27
  4.5 0.3 compare_reduce_fusion
  4.8 0.2 fusion
  5.0 0.1 copy.36
  5.1 0.1 copy_bitcast_fusion
  5.2 0.1 copy.38
  5.3 0.1 copy.29
  5.4 0.1 copy.33
  5.5 0.1 copy.31
  5.6 0.4 reduce_window_sum.11
  6.1 0.1 slice.7
  6.2 0.2 copy.32
  6.4 0.1 reshape_squeeze.3.count_ref
  6.5 0.1 broadcast_minimum_fusion
  6.5 1.0 select_reduce_fusion
  7.6 0.0 copy-start
  7.6 1.2 %copy-done = bf16[16,64,512]{2,1,0:T(8,128)(2,1)S(1)} copy-done((bf16[16,64,512]{2,1,0:T(8,128)(2,1)S(1)}, bf16[16,64,512]{2,1,0:T(8,128)(2,1)}, u32[]{:S(2)}) %copy-start) | copy-done | bytes 1048600
  8.8 65.8 %shard_map.28 = (bf16[7,8,512,128]{3,2,1,0:T(8,128)(2,1)S(1)}, bf16[2,16,64,512]{3,2,1,0:T(8,128)(2,1)S(1)}) custom-call(bf16[16,64,512]{2,1,0:T(8,128)(2,1)S(1)} %copy-done), custom_call_target="tpu_custom_call" | custom-call | tf_op jit(solution)/shard_map/pallas_call | solution.py:218
  74.6 20.2 %shard_map.29 = (bf16[16,512,1024]{2,1,0:T(8,128)(2,1)S(1)}, bf16[16,64,512]{2,1,0:T(8,128)(2,1)S(1)}) custom-call(s32[32]{0:T(128)S(1)} %reshape_squeeze.3.count_ref, s32[32,64]{1,0:T(8,128)S(1)} %bitcast.22, bf16[56,512,128]{2,1,0:T(8,128)(2,1)S(1)} %bitcast.21, bf16[2,16,64,512]{3,2,1,0:T(8,128)(2,1)S(1)} %get-tuple-element.10.left_ref), custom_call_target="tpu_custom_call" | custom-call | tf_op jit(solution)/shard_map/pallas_call | solution.py:369
  94.8 2.8 %shard_map.30.shared_ref = bf16[1,16,64,512]{3,2,1,0:T(8,128)(2,1)S(1)} custom-call(bf16[16,64,512]{2,1,0:T(8,128)(2,1)S(1)} %get-tuple-element.11.block.own_ref), custom_call_target="tpu_custom_call" | custom-call | tf_op jit(solution)/shard_map/pallas_call | solution.py:50
  97.6 8.3 %shard_map.31 = f32[16,64,512]{2,1,0:T(8,128)} custom-call(bf16[16,64,512]{2,1,0:T(8,128)(2,1)S(1)} %get-tuple-element.11.block.own_ref, bf16[1,16,64,512]{3,2,1,0:T(8,128)(2,1)S(1)} %shard_map.30.shared_ref, bf16[16,512,1024]{2,1,0:T(8,128)(2,1)S(1)} %get-tuple-element.12.rights), custom_call_target="tpu_custom_call" | custom-call | tf_op jit(solution)/shard_map/pallas_call | solution.py:380
  (6 shorter events, 0.1 us)
Async XLA Ops:
  7.6 1.2 %copy-start = (bf16[16,64,512]{2,1,0:T(8,128)(2,1)S(1)}, bf16[16,64,512]{2,1,0:T(8,128)(2,1)}, u32[]{:S(2)}) copy-start(bf16[16,64,512]{2,1,0:T(8,128)(2,1)} %block.1) | copy-start | bytes 3145732

commit v8 on v7

--- a/solution.py
+++ b/solution.py
@@ -10,6 +10,8 @@
 REACH = 48
 UNROLL = 8
 PIECES = 8
+CHUNKS = 8
+Z_FIRST = (0, 1, 3, 5, 7)
 LIMIT = 8 * 1024 * 1024
 
 
@@ -64,7 +66,7 @@
     turned[pair] = wide.T
 
 
-def direct_kernel(groups, size, span, block, panels, shared, turned, own_sem, col_send, col_recv, send_sem, recv_sem):
+def direct_kernel(groups, size, span, block, panels, shared, blank, turned, own_sem, col_send, col_recv, send_sem, recv_sem):
     me = lax.axis_index("row")
     offsets = [d for d in range(-span, span + 1) if d != 0]
     greet([{"row": lax.rem(me + d + size, size)} for d in offsets] + col_peers(groups))
@@ -80,12 +82,13 @@
             device_id={"row": lax.rem(me + d + size, size)}, device_id_type=pl.DeviceIdType.MESH,
         ))
         copies[-1].start()
+    blank[...] = jnp.zeros(blank.shape, blank.dtype)
     for copy in copies:
         copy.wait()
     own.wait()
 
 
-def relay_kernel(groups, size, chunks, block, panels, shared, turned, own_sem, col_send, col_recv, send_sem, recv_sem, held, up_send, up_recv):
+def relay_kernel(groups, size, chunks, block, panels, shared, blank, turned, own_sem, col_send, col_recv, send_sem, recv_sem, held, up_send, up_recv):
     me = lax.axis_index("row")
     x_step = 1 - 2 * lax.rem(me, 2)
     y_step = 2 - 4 * lax.rem(lax.div(me, 2), 2)
@@ -110,7 +113,7 @@
     def from_held(kind, chunk, way, slot, device):
         lines = pl.ds(chunk * depth, depth)
         copy = pltpu.make_async_remote_copy(
-            src_ref=held.at[way, chunk // 2], dst_ref=panels.at[slot, lines],
+            src_ref=held.at[way, Z_FIRST.index(chunk)], dst_ref=panels.at[slot, lines],
             send_sem=send_sem.at[kind, chunk], recv_sem=recv_sem.at[kind, chunk],
             device_id={"row": device}, device_id_type=pl.DeviceIdType.MESH,
         )
@@ -132,8 +135,8 @@
     def level(way, chunk):
         lines = pl.ds(chunk * depth, depth)
         return pltpu.make_async_remote_copy(
-            src_ref=turned.at[lines], dst_ref=held.at[way, chunk // 2],
-            send_sem=up_send.at[way, chunk // 2], recv_sem=up_recv.at[way, chunk // 2],
+            src_ref=turned.at[lines], dst_ref=held.at[way, Z_FIRST.index(chunk)],
+            send_sem=up_send.at[way, Z_FIRST.index(chunk)], recv_sem=up_recv.at[way, Z_FIRST.index(chunk)],
             device_id={"row": above if way == 0 else below}, device_id_type=pl.DeviceIdType.MESH,
         )
 
@@ -150,7 +153,7 @@
     for chunk in range(chunks):
         for pair in range(chunk * depth, (chunk + 1) * depth):
             turn(block, turned, pair)
-        if chunk % 2 == 0:
+        if chunk in Z_FIRST:
             on_level(chunk, lambda copy: copy.start())
         arriving.append((
             send(0, chunk, turned, 3 - x_step, x_near),
@@ -164,25 +167,28 @@
     lag = 2
     for chunk in range(chunks + lag):
         if chunk < chunks:
-            by_y = chunk % 4 != 1
+            by_y = chunk != 4
             arriving[chunk][0].wait_recv()
             if by_y:
                 corner[chunk] = send(2, chunk, panels.at[3 + x_step], 3 + x_step - y_step, y_near)
-            if chunk % 2 == 1:
+            if chunk not in Z_FIRST:
                 pass_on(0, chunk)
             arriving[chunk][1].wait_recv()
             if not by_y:
                 corner[chunk] = send(2, chunk, panels.at[3 + y_step], 3 + y_step - x_step, x_near)
-            if chunk % 2 == 1:
+            if chunk not in Z_FIRST:
                 pass_on(1, chunk)
             else:
                 on_level(chunk, lambda copy: copy.wait_recv())
                 late.append(from_held(3, chunk, x_held, 3 - x_step + 4 * x_sign, x_near))
                 spread[chunk] = from_held(4, chunk, y_held, 3 - y_step + 4 * y_sign, y_near)
+            lines = blank.shape[0] // chunks
+            for row in range(chunk * lines, (chunk + 1) * lines):
+                blank[row] = jnp.zeros(blank.shape[1:], blank.dtype)
         done = chunk - lag
         if done >= 0:
             corner[done].wait_recv()
-            if done % 2 == 1:
+            if done not in Z_FIRST:
                 pass_on(2, done)
             else:
                 spread[done].wait_recv()
@@ -190,7 +196,7 @@
                 late.append(send(5, done, panels.at[slot], slot - x_step, x_near))
     for copy in late:
         copy.wait_recv()
-    for chunk in range(0, chunks, 2):
+    for chunk in Z_FIRST:
         on_level(chunk, lambda copy: copy.wait_send())
     for copy in others:
         copy.wait_send()
@@ -200,7 +206,7 @@
 
 
 def fetch(density, groups, size, span, planes):
-    chunks = 8
+    chunks = CHUNKS
     if planes:
         body, shape = functools.partial(relay_kernel, groups, size, chunks), (6, chunks)
     else:
@@ -211,17 +217,18 @@
     extra = []
     if planes:
         extra = [
-            pltpu.VMEM((2, chunks // 2, rows // 2 // chunks, depth, 2 * width), density.dtype),
-            pltpu.SemaphoreType.DMA((2, chunks // 2)),
-            pltpu.SemaphoreType.DMA((2, chunks // 2)),
+            pltpu.VMEM((2, len(Z_FIRST), rows // 2 // chunks, depth, 2 * width), density.dtype),
+            pltpu.SemaphoreType.DMA((2, len(Z_FIRST))),
+            pltpu.SemaphoreType.DMA((2, len(Z_FIRST))),
         ]
-    panels, shared = pl.pallas_call(
+    panels, shared, blank = pl.pallas_call(
         body,
         in_specs=[inside],
-        out_specs=[inside, inside],
+        out_specs=[inside, inside, inside],
         out_shape=[
             jax.ShapeDtypeStruct((2 * span + 1,) + turned, density.dtype),
             jax.ShapeDtypeStruct((groups,) + density.shape, density.dtype),
+            jax.ShapeDtypeStruct((rows, depth, groups * depth), density.dtype),
         ],
         scratch_shapes=[
             pltpu.VMEM(turned, density.dtype),
@@ -235,7 +242,7 @@
             collective_id=0, has_side_effects=True, vmem_limit_bytes=LIMIT
         ),
     )(density)
-    return panels.reshape((-1,) + turned[1:]), shared
+    return panels.reshape((-1,) + turned[1:]), shared, blank
 
 
 def live_list(columns, rows, width, group_size, span):
@@ -293,13 +300,13 @@
     return total.T
 
 
-def first_kernel(stored, group_size, width, count_ref, code_ref, panels_ref, left_ref, rights, square_ref, halves_ref):
-    rows, depth, _ = rights.shape
+def first_kernel(stored, group_size, width, count_ref, code_ref, panels_ref, left_ref, blank_ref, rights, square_ref, halves_ref):
+    del blank_ref
+    rows = rights.shape[0]
     fill_halves(halves_ref, width)
 
     def one_row(row, carry):
         right_ref = rights.at[row]
-        right_ref[...] = jnp.zeros(right_ref.shape, right_ref.dtype)
         assemble(count_ref, code_ref, panels_ref, halves_ref, row, right_ref, width)
         total = multiply(right_ref, [left_ref.at[group, row] for group in range(left_ref.shape[0])])
         square_ref[row] = total.astype(square_ref.dtype)
@@ -363,12 +370,13 @@
     count, codes = live_list(columns, rows, width, group_size, span)
     size = lax.axis_size("row")
     planes = (size, groups, span) == (16, 2, 3)
-    panels, left = fetch(density, groups, size, span, planes)
+    panels, left, blank = fetch(density, groups, size, span, planes)
     inside = pl.BlockSpec(memory_space=pltpu.VMEM)
     scalars = pl.BlockSpec(memory_space=pltpu.SMEM)
     right, square = pl.pallas_call(
         functools.partial(first_kernel, stored, group_size, width),
-        in_specs=[scalars, scalars, inside, inside],
+        in_specs=[scalars, scalars, inside, inside, inside],
+        input_output_aliases={4: 0},
         out_specs=[inside, inside],
         out_shape=[
             jax.ShapeDtypeStruct((rows, depth, stored * width), density.dtype),
@@ -376,7 +384,7 @@
         ],
         scratch_shapes=[pltpu.VMEM((4, 2, width, 2 * width), density.dtype)],
         compiler_params=pltpu.CompilerParams(vmem_limit_bytes=LIMIT),
-    )(count, codes, panels, left)
+    )(count, codes, panels, left, blank)
     return pl.pallas_call(
         second_kernel,
         in_specs=[inside, inside, inside],

time: 106 us -> 108 us (1.019)
  Pallas kernels: 97.1 us -> 99.5 us
    pallas_call x1, Pallas kernels: 65.8 us -> 68.9 us  [fetch(): pl.pallas_call(body, in_specs=[inside], out_specs=[inside, inside, inside...]
where the time goes in v8:
time: 108 us
  Pallas kernels  99.5 us (92%)
  local copies, waits for them, and re-layouts  4.8 us (4%)
  other arithmetic  3.89 us (4%)
    pallas_call x1, Pallas kernels, fetch(): pl.pallas_call(body, in_specs=[inside], out_specs=[inside, inside, inside...  68.9 us
    pallas_call x1, Pallas kernels, shards(): pl.pallas_call(functools.partial(first_kernel, stored, group_size, width)...  19.4 us
    pallas_call x1, Pallas kernels, shards(): pl.pallas_call(second_kernel, in_specs=[inside, inside, inside], out_spec...  8.35 us
    pallas_call x1, Pallas kernels, exchange(): pl.pallas_call(functools.partial(exchange_kernel, groups), in_specs=[pl.B...  2.82 us

profile of v8, /device:TPU:0, one launch (start us, length us, event | category | flops | bytes accessed | tf_op | source)
XLA Modules:
  0.0 108.3 jit_solution(5056560963516287962)
XLA Ops:
  0.0 0.8 dynamic_slice.11
  0.8 0.1 copy.29
  0.9 0.7 constant_dynamic-slice_fusion
  1.6 0.8 compare_and_fusion
  2.4 0.1 copy.25
  2.5 0.1 copy.27
  2.6 0.1 reshape.131
  2.7 0.8 fusion.2
  3.5 0.1 copy.41
  3.6 0.7 gather_fusion
  4.3 0.1 broadcast_select_fusion
  4.4 0.1 copy.28
  4.5 0.3 compare_reduce_fusion
  4.8 0.2 fusion
  5.0 0.1 copy.37
  5.1 0.1 copy_bitcast_fusion
  5.2 0.1 copy.39
  5.3 0.1 copy.30
  5.4 0.1 copy.34
  5.6 0.1 copy.32
  5.6 0.4 reduce_window_sum.11
  6.1 0.1 slice.7
  6.2 0.2 copy.33
  6.4 0.1 reshape_squeeze.3.count_ref
  6.5 0.1 broadcast_minimum_fusion
  6.5 1.0 select_reduce_fusion
  7.6 0.0 copy-start
  7.6 1.2 %copy-done = bf16[16,64,512]{2,1,0:T(8,128)(2,1)S(1)} copy-done((bf16[16,64,512]{2,1,0:T(8,128)(2,1)S(1)}, bf16[16,64,512]{2,1,0:T(8,128)(2,1)}, u32[]{:S(2)}) %copy-start) | copy-done | bytes 1048600
  8.8 68.9 %shard_map.28 = (bf16[7,8,512,128]{3,2,1,0:T(8,128)(2,1)S(1)}, bf16[2,16,64,512]{3,2,1,0:T(8,128)(2,1)S(1)}, bf16[16,512,1024]{2,1,0:T(8,128)(2,1)S(1)}) custom-call(bf16[16,64,512]{2,1,0:T(8,128)(2,1)S(1)} %copy-done), custom_call_target="tpu_custom_call" | custom-call | tf_op jit(solution)/shard_map/pallas_call | solution.py:224
  77.7 19.4 %shard_map.29 = (bf16[16,512,1024]{2,1,0:T(8,128)(2,1)S(1)}, bf16[16,64,512]{2,1,0:T(8,128)(2,1)S(1)}) custom-call(s32[32]{0:T(128)S(1)} %reshape_squeeze.3.count_ref, s32[32,64]{1,0:T(8,128)S(1)} %bitcast.22, bf16[56,512,128]{2,1,0:T(8,128)(2,1)S(1)} %bitcast.21, ...), custom_call_target="tpu_custom_call", output_to_operand_aliasing={{0}: (4, {})} | custom-call | tf_op jit(solution)/shard_map/pallas_call | solution.py:376
  97.2 2.8 %shard_map.30.shared_ref = bf16[1,16,64,512]{3,2,1,0:T(8,128)(2,1)S(1)} custom-call(bf16[16,64,512]{2,1,0:T(8,128)(2,1)S(1)} %get-tuple-element.13.block.own_ref), custom_call_target="tpu_custom_call" | custom-call | tf_op jit(solution)/shard_map/pallas_call | solution.py:52
  100.0 8.3 %shard_map.31 = f32[16,64,512]{2,1,0:T(8,128)} custom-call(bf16[16,64,512]{2,1,0:T(8,128)(2,1)S(1)} %get-tuple-element.13.block.own_ref, bf16[1,16,64,512]{3,2,1,0:T(8,128)(2,1)S(1)} %shard_map.30.shared_ref, bf16[16,512,1024]{2,1,0:T(8,128)(2,1)S(1)} %get-tuple-element.14.rights), custom_call_target="tpu_custom_call" | custom-call | tf_op jit(solution)/shard_map/pallas_call | solution.py:388
  (6 shorter events, 0.1 us)
Async XLA Ops:
  7.6 1.2 %copy-start = (bf16[16,64,512]{2,1,0:T(8,128)(2,1)S(1)}, bf16[16,64,512]{2,1,0:T(8,128)(2,1)}, u32[]{:S(2)}) copy-start(bf16[16,64,512]{2,1,0:T(8,128)(2,1)} %block.1) | copy-start | bytes 3145732

commit v9 on v7

--- a/solution.py
+++ b/solution.py
@@ -297,15 +297,19 @@
     rows, depth, _ = rights.shape
     fill_halves(halves_ref, width)
 
-    def one_row(row, carry):
+    def fill(row, carry):
         right_ref = rights.at[row]
         right_ref[...] = jnp.zeros(right_ref.shape, right_ref.dtype)
         assemble(count_ref, code_ref, panels_ref, halves_ref, row, right_ref, width)
-        total = multiply(right_ref, [left_ref.at[group, row] for group in range(left_ref.shape[0])])
+        return carry
+
+    def one_row(row, carry):
+        total = multiply(rights.at[row], [left_ref.at[group, row] for group in range(left_ref.shape[0])])
         square_ref[row] = total.astype(square_ref.dtype)
         return carry
 
-    lax.fori_loop(0, rows, one_row, 0)
+    lax.fori_loop(0, rows, fill, 0)
+    lax.fori_loop(0, rows, one_row, 0, unroll=4)
 
 
 def second_kernel(own_ref, shared_ref, rights, out_hbm, out_ref, out_sem):
@@ -324,7 +328,7 @@
         leave(row).wait()
         return carry
 
-    lax.fori_loop(0, rows, one_row, 0)
+    lax.fori_loop(0, rows, one_row, 0, unroll=4)
     lax.fori_loop(0, rows, done, 0)
 
 

time: 106 us -> 102 us (0.962)
  Pallas kernels: 97.1 us -> 92.1 us
    pallas_call x1, Pallas kernels: 20.2 us -> 17.4 us  [shards(): pl.pallas_call(functools.partial(first_kernel, stored, group_size, width)...]
    pallas_call x1, Pallas kernels: 8.35 us -> 6.1 us  [shards(): pl.pallas_call(second_kernel, in_specs=[inside, inside, inside], out_spec...]
where the time goes in v9:
time: 102 us; the launch traced here: 101 us
  Pallas kernels  92.1 us (90%)
  local copies, waits for them, and re-layouts  4.8 us (5%)
  other arithmetic  3.89 us (4%)
    pallas_call x1, Pallas kernels, fetch(): pl.pallas_call(body, in_specs=[inside], out_specs=[inside, inside], out_s...  65.8 us
    pallas_call x1, Pallas kernels, shards(): pl.pallas_call(functools.partial(first_kernel, stored, group_size, width)...  17.4 us
    pallas_call x1, Pallas kernels, shards(): pl.pallas_call(second_kernel, in_specs=[inside, inside, inside], out_spec...  6.1 us
    pallas_call x1, Pallas kernels, exchange(): pl.pallas_call(functools.partial(exchange_kernel, groups), in_specs=[pl.B...  2.82 us

profile of v9, /device:TPU:0, one launch (start us, length us, event | category | flops | bytes accessed | tf_op | source)
XLA Modules:
  0.0 100.9 jit_solution(4026954366764281487)
XLA Ops:
  0.0 0.8 dynamic_slice.11
  0.8 0.1 copy.28
  0.9 0.7 constant_dynamic-slice_fusion
  1.6 0.8 compare_and_fusion
  2.4 0.1 copy.24
  2.5 0.1 copy.26
  2.6 0.1 reshape.131
  2.7 0.8 fusion.2
  3.5 0.1 copy.40
  3.6 0.7 gather_fusion
  4.3 0.1 broadcast_select_fusion
  4.4 0.1 copy.27
  4.5 0.3 compare_reduce_fusion
  4.8 0.2 fusion
  5.0 0.1 copy.36
  5.1 0.1 copy_bitcast_fusion
  5.2 0.1 copy.38
  5.3 0.1 copy.29
  5.4 0.1 copy.33
  5.6 0.1 copy.31
  5.6 0.4 reduce_window_sum.11
  6.1 0.1 slice.7
  6.2 0.2 copy.32
  6.4 0.1 reshape_squeeze.3.count_ref
  6.5 0.1 broadcast_minimum_fusion
  6.5 1.0 %select_reduce_fusion = s32[16,2,64]{2,1,0:T(2,128)S(1)} fusion(s32[16,2,64]{2,1,0:T(2,128)S(1)} %copy.38, s32[16,2,64]{2,1,0:T(2,128)S(1)} %broadcast_minimum_fusion, s32[16,2,64]{2,1,0:T(2,128)S(1)} %copy.34, pred[16,2,64]{2,1,0:T(4,128)(4,1)S(1)} %copy.33), kind=kLoop, calls=%fused_computation.1 | loop fusion | flops 522240 | bytes 34816 | tf_op jit(solution)/shard_map/reduce_sum | solution.py:270
  7.6 0.0 copy-start
  7.6 1.2 %copy-done = bf16[16,64,512]{2,1,0:T(8,128)(2,1)S(1)} copy-done((bf16[16,64,512]{2,1,0:T(8,128)(2,1)S(1)}, bf16[16,64,512]{2,1,0:T(8,128)(2,1)}, u32[]{:S(2)}) %copy-start) | copy-done | bytes 1048600
  8.8 65.8 %shard_map.28 = (bf16[7,8,512,128]{3,2,1,0:T(8,128)(2,1)S(1)}, bf16[2,16,64,512]{3,2,1,0:T(8,128)(2,1)S(1)}) custom-call(bf16[16,64,512]{2,1,0:T(8,128)(2,1)S(1)} %copy-done), custom_call_target="tpu_custom_call" | custom-call | tf_op jit(solution)/shard_map/pallas_call | solution.py:218
  74.6 17.4 %shard_map.29 = (bf16[16,512,1024]{2,1,0:T(8,128)(2,1)S(1)}, bf16[16,64,512]{2,1,0:T(8,128)(2,1)S(1)}) custom-call(s32[32]{0:T(128)S(1)} %reshape_squeeze.3.count_ref, s32[32,64]{1,0:T(8,128)S(1)} %bitcast.22, bf16[56,512,128]{2,1,0:T(8,128)(2,1)S(1)} %bitcast.21, bf16[2,16,64,512]{3,2,1,0:T(8,128)(2,1)S(1)} %get-tuple-element.10.left_ref), custom_call_target="tpu_custom_call" | custom-call | tf_op jit(solution)/shard_map/pallas_call | solution.py:373
  92.0 2.8 %shard_map.30.shared_ref = bf16[1,16,64,512]{3,2,1,0:T(8,128)(2,1)S(1)} custom-call(bf16[16,64,512]{2,1,0:T(8,128)(2,1)S(1)} %get-tuple-element.11.block.own_ref), custom_call_target="tpu_custom_call" | custom-call | tf_op jit(solution)/shard_map/pallas_call | solution.py:50
  94.8 6.1 %shard_map.31 = f32[16,64,512]{2,1,0:T(8,128)} custom-call(bf16[16,64,512]{2,1,0:T(8,128)(2,1)S(1)} %get-tuple-element.11.block.own_ref, bf16[1,16,64,512]{3,2,1,0:T(8,128)(2,1)S(1)} %shard_map.30.shared_ref, bf16[16,512,1024]{2,1,0:T(8,128)(2,1)S(1)} %get-tuple-element.12.rights), custom_call_target="tpu_custom_call" | custom-call | tf_op jit(solution)/shard_map/pallas_call | solution.py:384
  (6 shorter events, 0.1 us)
Async XLA Ops:
  7.6 1.2 %copy-start = (bf16[16,64,512]{2,1,0:T(8,128)(2,1)S(1)}, bf16[16,64,512]{2,1,0:T(8,128)(2,1)}, u32[]{:S(2)}) copy-start(bf16[16,64,512]{2,1,0:T(8,128)(2,1)} %block.1) | copy-start | bytes 3145732

commit v10 on v9

--- a/solution.py
+++ b/solution.py
@@ -344,7 +344,7 @@
                 place, inner = (code >> 2) & 15, (code >> 6) & 255
                 slot, source = (code >> 14) & 255, code >> 22
                 value = panels_ref[source, pl.ds(pl.multiple_of(slot * width, width), width), :]
-                swapped = jnp.concatenate([value[:, width:], value[:, :width]], axis=1)
+                swapped = pltpu.roll(value, width, 1)
                 value = value * halves_ref[kind, 0] + swapped * halves_ref[kind, 1]
                 lanes = pl.ds(pl.multiple_of(inner * 2 * width, 2 * width), 2 * width)
                 lines = pl.ds(pl.multiple_of(place * width, width), width)

time: 102 us -> 102 us (level)
  no operation moved by 1% of the time
where the time goes in v10:
time: 102 us; the launch traced here: 101 us
  Pallas kernels  92.6 us (91%)
  local copies, waits for them, and re-layouts  4.8 us (5%)
  other arithmetic  3.89 us (4%)
    pallas_call x1, Pallas kernels, fetch(): pl.pallas_call(body, in_specs=[inside], out_specs=[inside, inside], out_s...  65.8 us
    pallas_call x1, Pallas kernels, shards(): pl.pallas_call(functools.partial(first_kernel, stored, group_size, width)...  17.9 us
    pallas_call x1, Pallas kernels, shards(): pl.pallas_call(second_kernel, in_specs=[inside, inside, inside], out_spec...  6.11 us
    pallas_call x1, Pallas kernels, exchange(): pl.pallas_call(functools.partial(exchange_kernel, groups), in_specs=[pl.B...  2.82 us

profile of v10, /device:TPU:0, one launch (start us, length us, event | category | flops | bytes accessed | tf_op | source)
XLA Modules:
  0.0 101.4 jit_solution(4026954366764281487)
XLA Ops:
  0.0 0.8 dynamic_slice.11
  0.8 0.1 copy.28
  0.9 0.7 constant_dynamic-slice_fusion
  1.6 0.8 compare_and_fusion
  2.4 0.1 copy.24
  2.5 0.1 copy.26
  2.6 0.1 reshape.131
  2.7 0.8 fusion.2
  3.5 0.1 copy.40
  3.6 0.7 gather_fusion
  4.3 0.1 broadcast_select_fusion
  4.4 0.1 copy.27
  4.5 0.3 compare_reduce_fusion
  4.8 0.2 fusion
  5.0 0.1 copy.36
  5.1 0.1 copy_bitcast_fusion
  5.2 0.1 copy.38
  5.3 0.1 copy.29
  5.4 0.1 copy.33
  5.5 0.1 copy.31
  5.6 0.4 reduce_window_sum.11
  6.1 0.1 slice.7
  6.2 0.2 copy.32
  6.4 0.1 reshape_squeeze.3.count_ref
  6.5 0.1 broadcast_minimum_fusion
  6.5 1.0 %select_reduce_fusion = s32[16,2,64]{2,1,0:T(2,128)S(1)} fusion(s32[16,2,64]{2,1,0:T(2,128)S(1)} %copy.38, s32[16,2,64]{2,1,0:T(2,128)S(1)} %broadcast_minimum_fusion, s32[16,2,64]{2,1,0:T(2,128)S(1)} %copy.34, pred[16,2,64]{2,1,0:T(4,128)(4,1)S(1)} %copy.33), kind=kLoop, calls=%fused_computation.1 | loop fusion | flops 522240 | bytes 34816 | tf_op jit(solution)/shard_map/reduce_sum | solution.py:270
  7.6 0.0 copy-start
  7.6 1.2 %copy-done = bf16[16,64,512]{2,1,0:T(8,128)(2,1)S(1)} copy-done((bf16[16,64,512]{2,1,0:T(8,128)(2,1)S(1)}, bf16[16,64,512]{2,1,0:T(8,128)(2,1)}, u32[]{:S(2)}) %copy-start) | copy-done | bytes 1048600
  8.8 65.8 %shard_map.28 = (bf16[7,8,512,128]{3,2,1,0:T(8,128)(2,1)S(1)}, bf16[2,16,64,512]{3,2,1,0:T(8,128)(2,1)S(1)}) custom-call(bf16[16,64,512]{2,1,0:T(8,128)(2,1)S(1)} %copy-done), custom_call_target="tpu_custom_call" | custom-call | tf_op jit(solution)/shard_map/pallas_call | solution.py:218
  74.6 17.9 %shard_map.29 = (bf16[16,512,1024]{2,1,0:T(8,128)(2,1)S(1)}, bf16[16,64,512]{2,1,0:T(8,128)(2,1)S(1)}) custom-call(s32[32]{0:T(128)S(1)} %reshape_squeeze.3.count_ref, s32[32,64]{1,0:T(8,128)S(1)} %bitcast.22, bf16[56,512,128]{2,1,0:T(8,128)(2,1)S(1)} %bitcast.21, bf16[2,16,64,512]{3,2,1,0:T(8,128)(2,1)S(1)} %get-tuple-element.10.left_ref), custom_call_target="tpu_custom_call" | custom-call | tf_op jit(solution)/shard_map/pallas_call | solution.py:373
  92.5 2.8 %shard_map.30.shared_ref = bf16[1,16,64,512]{3,2,1,0:T(8,128)(2,1)S(1)} custom-call(bf16[16,64,512]{2,1,0:T(8,128)(2,1)S(1)} %get-tuple-element.11.block.own_ref), custom_call_target="tpu_custom_call" | custom-call | tf_op jit(solution)/shard_map/pallas_call | solution.py:50
  95.3 6.1 %shard_map.31 = f32[16,64,512]{2,1,0:T(8,128)} custom-call(bf16[16,64,512]{2,1,0:T(8,128)(2,1)S(1)} %get-tuple-element.11.block.own_ref, bf16[1,16,64,512]{3,2,1,0:T(8,128)(2,1)S(1)} %shard_map.30.shared_ref, bf16[16,512,1024]{2,1,0:T(8,128)(2,1)S(1)} %get-tuple-element.12.rights), custom_call_target="tpu_custom_call" | custom-call | tf_op jit(solution)/shard_map/pallas_call | solution.py:384
  (6 shorter events, 0.1 us)
Async XLA Ops:
  7.6 1.2 %copy-start = (bf16[16,64,512]{2,1,0:T(8,128)(2,1)S(1)}, bf16[16,64,512]{2,1,0:T(8,128)(2,1)}, u32[]{:S(2)}) copy-start(bf16[16,64,512]{2,1,0:T(8,128)(2,1)} %block.1) | copy-start | bytes 3145732
